TPU v7x, 512 devices: a whole 4x8x8 slice. The times are simulated.
512 devices in a mesh: seq: 64 (over y_lo, z, x), head: 8 (over y_hi, core).
Axes of the slice: x: 4, y: 8 (y_hi: 4, y_lo: 2; y = y_hi * 2 + y_lo), z: 8, core: 2. Of those that a mesh axis runs over, the one named last changes fastest.
Arguments:
- qkv: bfloat16 [3, 32768, 3072], P(None, ('seq', 'head')), may hold values from -6 to 6
- text_kv: bfloat16 [2, 256, 3072], P(None, None, 'head'), may hold values from -6 to 6
- window_mask: int32 [128, 27], P('seq'), may hold values from 0 to 1, as said below
Outputs:
- attended: bfloat16 [32768, 3072], P(('seq', 'head'))
Inputs may be any that keep to these rules, and one draw needn't show every extreme that they name: `window_mask`: each entry is 1 for offset 13 (the query's own tile) and 0 wherever the offset leads outside the grid.
All inputs are finite; a program needn't handle non-finite values.
Results may differ from a plain program's by a relative error of at most 0.0049.
Values may be sent and summed in bfloat16 or wider, within the bound.
A program may use at most 128 MiB of HBM per device.

v0:
```python
import math

import jax
import jax.numpy as jnp
from jax import lax
from jax.sharding import PartitionSpec as P

HEAD_DIM = 128
GW = 8


def from_behind(block, axis, distance):
    devices = range(lax.axis_size(axis))
    route = [(i - distance, i) for i in devices if i - distance in devices]
    return lax.ppermute(block, axis, route)


def visible_tiles(mask_rows, count):
    query_tile = jnp.arange(count, dtype=jnp.int32)[:, None, None]
    piece = jnp.arange(9, dtype=jnp.int32)[None, :, None]
    key_tile = jnp.arange(count, dtype=jnp.int32)[None, None, :]
    delta = key_tile - query_tile
    offset = (delta + 1) * 9 + piece
    table = (offset[..., None] == jnp.arange(27, dtype=jnp.int32)).astype(jnp.int32)
    picked = jnp.sum(table * mask_rows[:, None, None, :], axis=-1)
    usable = (picked > 0) & (jnp.abs(delta) <= 1)
    return jnp.transpose(usable, (1, 0, 2))


def neighbor_pull(pairs, steps):
    return from_behind(pairs, "seq", steps)


def on_device(qkv, text_kv, window_mask):
    local = lax.all_to_all(qkv, "head", split_axis=2, concat_axis=1, tiled=True)
    query = local[0]
    pairs = local[1:]
    rows = query.shape[0]
    features = query.shape[1]
    heads_dev = features // HEAD_DIM
    tile_count = window_mask.shape[0]
    tile_len = rows // tile_count
    collected = []
    for row_step in (-1, 0, 1):
        for col_step in (-1, 0, 1):
            if row_step == 0 and col_step == 0:
                collected.append(pairs)
            else:
                collected.append(neighbor_pull(pairs, -(row_step * GW + col_step)))
    pieces = jnp.stack(collected)
    keys_all = pieces[:, 0].reshape(9, rows, heads_dev, HEAD_DIM)
    vals_all = pieces[:, 1].reshape(9, rows, heads_dev, HEAD_DIM)
    tiles = visible_tiles(window_mask, tile_count)
    allowed_all = jnp.repeat(jnp.repeat(tiles, tile_len, axis=1), tile_len, axis=2)
    query3 = query.reshape(rows, heads_dev, HEAD_DIM)
    text_len = text_kv.shape[1]
    text_keys = text_kv[0].reshape(text_len, heads_dev, HEAD_DIM)
    text_vals = text_kv[1].reshape(text_len, heads_dev, HEAD_DIM)
    scale = 1.0 / math.sqrt(HEAD_DIM)
    block = math.gcd(rows, 256)
    blocks = rows // block

    def query_block(index):
        first = index * block
        part_q = lax.dynamic_slice_in_dim(query3, first, block, 0)
        part_allowed = lax.dynamic_slice_in_dim(allowed_all, first, block, 1)
        text_score = (
            jnp.einsum("qhd,khd->hqk", part_q, text_keys, preferred_element_type=jnp.float32)
            * scale
        )
        video_score = (
            jnp.einsum("qhd,pkhd->phqk", part_q, keys_all, preferred_element_type=jnp.float32)
            * scale
        )
        video_score = jnp.where(part_allowed[:, None], video_score, -1e30)
        largest = jnp.maximum(jnp.max(text_score, axis=-1), jnp.max(video_score, axis=(0, 3)))
        total = jnp.sum(jnp.exp(text_score - largest[..., None]), axis=-1)
        total = total + jnp.sum(jnp.exp(video_score - largest[None, ..., None]), axis=(0, 3))

        def weights_of(score):
            return (jnp.exp(score - largest[..., None]) / total[..., None]).astype(jnp.bfloat16)

        start_acc = jnp.einsum(
            "hqk,khd->qhd", weights_of(text_score), text_vals, preferred_element_type=jnp.float32
        )

        def accumulate(acc, item):
            score, vals3 = item
            return (
                acc
                + jnp.einsum(
                    "hqk,khd->qhd", weights_of(score), vals3, preferred_element_type=jnp.float32
                ),
                None,
            )

        summed, _ = lax.scan(accumulate, start_acc, (video_score, vals_all))
        return summed.reshape(block, features).astype(jnp.bfloat16)

    result = lax.map(query_block, jnp.arange(blocks, dtype=jnp.int32)).reshape(rows, features)
    return lax.all_to_all(result, "head", split_axis=0, concat_axis=1, tiled=True)


def solution(mesh):
    placed = (P(None, ("seq", "head"), None), P(None, None, "head"), P("seq", None))
    return jax.shard_map(
        on_device, mesh=mesh, in_specs=placed, out_specs=P(("seq", "head"), None), check_vma=False
    )
```

profile of v0, /device:TPU:6, one launch (start us, length us, event | category | flops | bytes accessed | tf_op | source)
XLA Modules:
  0.0 384.5 jit_solution(3527115965230962056)
XLA Ops:
  0.0 4.6 %copy.73 = bf16[3,64,3072]{1,0,2:T(4,128)(2,1)S(1)} copy(bf16[3,64,3072]{2,1,0:T(8,128)(2,1)} %param.7) | data formatting | bytes 2359296 | tf_op args[0]
  4.6 4.1 %reshape.84 = bf16[8,2,36864]{2,1,0:T(2,128)(2,1)} reshape(bf16[3072,3,64]{2,1,0:T(4,128)(2,1)S(1)} %bitcast.95) | data formatting | bytes 2359296
  8.6 7.2 %all-to-all-start = ((bf16[8,2,36864]{2,1,0:T(2,128)(2,1)}), bf16[8,2,36864]{2,1,0:T(2,128)(2,1)}, u32[]{:S(2)}, u32[]{:S(2)}) async-start(bf16[8,2,36864]{2,1,0:T(2,128)(2,1)} %reshape.84), calls=%async_computation | async-start | bytes 2359296 | tf_op jit(solution)/shard_map/all_to_all | solution.py:35
  15.9 31.9 %all-to-all-done = bf16[8,2,36864]{2,1,0:T(2,128)(2,1)} async-done(((bf16[8,2,36864]{2,1,0:T(2,128)(2,1)}), bf16[8,2,36864]{2,1,0:T(2,128)(2,1)}, u32[]{:S(2)}, u32[]{:S(2)}) %all-to-all-start) | async-done | bytes 1179680 | tf_op jit(solution)/shard_map/all_to_all | solution.py:35
  47.8 5.1 %reshape.85 = bf16[3072,3,64]{2,1,0:T(4,128)(2,1)S(1)} reshape(bf16[8,2,36864]{2,1,0:T(2,128)(2,1)} %all-to-all-done) | data formatting | bytes 2359296
  56.8 8.7 %collective-permute-start = (bf16[2,512,384]{2,1,0:T(8,128)(2,1)S(1)}, bf16[2,512,384]{2,1,0:T(8,128)(2,1)}, u32[]{:S(2)}, u32[]{:S(2)}) collective-permute-start(bf16[2,512,384]{2,1,0:T(8,128)(2,1)S(1)} %bitcast.99), channel_id=1, source_target_pairs={{0,72},{8,80},{16,88},{24,96},{32,104},{40,112},{48,120},{56,128},... | collective-permute-start | bytes 2359304 | tf_op jit(solution)/shard_map/ppermute | solution.py:15
  66.0 5.5 %collective-permute-start.1 = (bf16[2,512,384]{2,1,0:T(8,128)(2,1)S(1)}, bf16[2,512,384]{2,1,0:T(8,128)(2,1)S(1)}, u32[]{:S(2)}, u32[]{:S(2)}) collective-permute-start(bf16[2,512,384]{2,1,0:T(8,128)(2,1)S(1)} %bitcast.100), channel_id=1, source_target_pairs={{0,64},{8,72},{16,80},{24,88},{32,96},{40,104},{48,112},{56,120},{... | collective-permute-start | bytes 2359304 | tf_op jit(solution)/shard_map/ppermute | solution.py:15
  72.6 4.4 %collective-permute-start.2 = (bf16[2,512,384]{2,1,0:T(8,128)(2,1)S(1)}, bf16[2,512,384]{2,1,0:T(8,128)(2,1)S(1)}, u32[]{:S(2)}, u32[]{:S(2)}) collective-permute-start(bf16[2,512,384]{2,1,0:T(8,128)(2,1)S(1)} %bitcast.101), channel_id=1, source_target_pairs={{0,56},{8,64},{16,72},{24,80},{32,88},{40,96},{48,104},{56,112},{6... | collective-permute-start | bytes 2359304 | tf_op jit(solution)/shard_map/ppermute | solution.py:15
  79.9 4.5 %collective-permute-start.3 = (bf16[2,512,384]{2,1,0:T(8,128)(2,1)S(1)}, bf16[2,512,384]{2,1,0:T(8,128)(2,1)}, u32[]{:S(2)}, u32[]{:S(2)}) collective-permute-start(bf16[2,512,384]{2,1,0:T(8,128)(2,1)S(1)} %bitcast.102), channel_id=1, source_target_pairs={{0,8},{8,16},{16,24},{24,32},{32,40},{40,48},{48,56},{56,64},{64,7... | collective-permute-start | bytes 2359304 | tf_op jit(solution)/shard_map/ppermute | solution.py:15
  90.9 8.6 %collective-permute-done.1 = bf16[2,512,384]{2,1,0:T(8,128)(2,1)S(1)} collective-permute-done((bf16[2,512,384]{2,1,0:T(8,128)(2,1)S(1)}, bf16[2,512,384]{2,1,0:T(8,128)(2,1)S(1)}, u32[]{:S(2)}, u32[]{:S(2)}) %collective-permute-start.1) | collective-permute-done | bytes 786464 | tf_op jit(solution)/shard_map/ppermute | solution.py:15
  101.0 15.4 %collective-permute-done.2 = bf16[2,512,384]{2,1,0:T(8,128)(2,1)S(1)} collective-permute-done((bf16[2,512,384]{2,1,0:T(8,128)(2,1)S(1)}, bf16[2,512,384]{2,1,0:T(8,128)(2,1)S(1)}, u32[]{:S(2)}, u32[]{:S(2)}) %collective-permute-start.2) | collective-permute-done | bytes 786464 | tf_op jit(solution)/shard_map/ppermute | solution.py:15
  118.1 25.0 %collective-permute-done.3 = bf16[2,512,384]{2,1,0:T(8,128)(2,1)} collective-permute-done((bf16[2,512,384]{2,1,0:T(8,128)(2,1)S(1)}, bf16[2,512,384]{2,1,0:T(8,128)(2,1)}, u32[]{:S(2)}, u32[]{:S(2)}) %collective-permute-start.3) | collective-permute-done | bytes 786464 | tf_op jit(solution)/shard_map/ppermute | solution.py:15
  146.0 49.1 %collective-permute-done.6 = bf16[2,512,384]{2,1,0:T(8,128)(2,1)S(1)} collective-permute-done((bf16[2,512,384]{2,1,0:T(8,128)(2,1)S(1)}, bf16[2,512,384]{2,1,0:T(8,128)(2,1)S(1)}, u32[]{:S(2)}, u32[]{:S(2)}) %collective-permute-start.6) | collective-permute-done | bytes 786464 | tf_op jit(solution)/shard_map/ppermute | solution.py:15
  195.2 64.2 %collective-permute-done.7 = bf16[2,512,384]{2,1,0:T(8,128)(2,1)S(1)} collective-permute-done((bf16[2,512,384]{2,1,0:T(8,128)(2,1)S(1)}, bf16[2,512,384]{2,1,0:T(8,128)(2,1)S(1)}, u32[]{:S(2)}, u32[]{:S(2)}) %collective-permute-start.7) | collective-permute-done | bytes 786464 | tf_op jit(solution)/shard_map/ppermute | solution.py:15
  262.1 5.7 %copy.81 = bf16[9,1,512,384]{2,3,0,1:T(8,128)(2,1)} copy(bf16[9,1,512,384]{3,2,1,0:T(8,128)(2,1)} %get-tuple-element.186) | data formatting | bytes 7077888 | tf_op jit(solution)/shard_map/slice | solution.py:51
  267.8 5.8 %copy.87 = bf16[9,512,3,128]{3,1,0,2:T(8,128)(2,1)} copy(bf16[9,512,3,128]{1,3,2,0:T(8,128)(2,1)} %bitcast.93) | data formatting | bytes 7077888 | tf_op jit(solution)/shard_map/while | solution.py:100
  278.6 85.4 %while.21 = (s32[]{:T(128)}, bf16[2,256,384]{2,1,0:T(8,128)(2,1)}, s32[2]{0:T(128)S(1)}, bf16[512,3,128]{2,0,1:T(8,128)(2,1)}, bf16[256,3,128]{2,0,1:T(8,128)(2,...) while((s32[]{:T(128)}, bf16[2,256,384]{2,1,0:T(8,128)(2,1)}, ...), condition=%wide.region_8.9_spmd, body=%wide.region_1.8_spmd.sunk | while | flops 1127741952 | bytes 71419424 | solution.py:100
  282.3 10.1 %fusion.35 = (f32[3,256]{1,0:T(4,128)S(1)}, f32[9,3,256,512]{3,2,0,1:T(8,128)}) fusion(bf16[9,512,3,128]{3,1,0,2:T(8,128)(2,1)} %get-tuple-element.359, bf16[512,3,128]{2,0,1:T(8,128)(2,1)} %get-tuple-element.356, s32[]{:T(128)S(6)} %select_n.10, pred[9,256,512]{2,1,0:T(8,128)(4,1)S(1)} %copy.104), kind=kOutput, calls=%fused_computation.40.clone.1 | convolution fusion | flops 916585728 | bytes 19074052 | tf_op jit(solution)/shard_map/while/body/eval_jaxpr/qhd,pkhd->phqk/dot_general | solution.py:72
  292.8 7.1 %exponential_reduce_fusion.2 = f32[3,256]{1,0:T(4,128)S(1)} fusion(f32[9,3,256,512]{3,2,0,1:T(8,128)} %get-tuple-element.307, f32[3,256]{1,0:T(4,128)S(1)} %max.12), kind=kLoop, calls=%fused_computation.10.clone.1 | loop fusion | flops 7077120 | bytes 14161920 | tf_op jit(solution)/shard_map/while/body/eval_jaxpr/reduce_sum | solution.py:78
  300.5 19.8 %while.22 = (s32[]{:T(128)}, f32[256,3,128]{0,2,1:T(8,128)S(1)}, bf16[9,512,3,128]{1,3,2,0:T(8,128)(2,1)}, f32[9,3,256,512]{3,2,0,1:T(8,128)}, f32[3,256]{1,0:T(4,128)S(1)}, /*index=5*/f32[3,256]{1,0:T(4,128)S(1)}, s32[]{:T(128)}) while((s32[]{:T(128)}, f32[256,3,128]{0,2,1:T(8,128)S(1)}, bf16[9,512,3,128]{1,3,2,0:T(8,128)(2,1)}, ...), condition=%wide.region_7.7_spmd, body=%wide.region_6.6_spmd.sunk | while | flops 101941248 | bytes 2759757 | solution.py:97
  325.0 10.1 %fusion.35 = (f32[3,256]{1,0:T(4,128)S(1)}, f32[9,3,256,512]{3,2,0,1:T(8,128)}) fusion(bf16[9,512,3,128]{3,1,0,2:T(8,128)(2,1)} %get-tuple-element.359, bf16[512,3,128]{2,0,1:T(8,128)(2,1)} %get-tuple-element.356, s32[]{:T(128)S(6)} %select_n.10, pred[9,256,512]{2,1,0:T(8,128)(4,1)S(1)} %copy.104), kind=kOutput, calls=%fused_computation.40.clone.1 | convolution fusion | flops 916585728 | bytes 19074052 | tf_op jit(solution)/shard_map/while/body/eval_jaxpr/qhd,pkhd->phqk/dot_general | solution.py:72
  335.5 7.1 %exponential_reduce_fusion.2 = f32[3,256]{1,0:T(4,128)S(1)} fusion(f32[9,3,256,512]{3,2,0,1:T(8,128)} %get-tuple-element.307, f32[3,256]{1,0:T(4,128)S(1)} %max.12), kind=kLoop, calls=%fused_computation.10.clone.1 | loop fusion | flops 7077120 | bytes 14161920 | tf_op jit(solution)/shard_map/while/body/eval_jaxpr/reduce_sum | solution.py:78
  343.2 19.8 %while.22 = (s32[]{:T(128)}, f32[256,3,128]{0,2,1:T(8,128)S(1)}, bf16[9,512,3,128]{1,3,2,0:T(8,128)(2,1)}, f32[9,3,256,512]{3,2,0,1:T(8,128)}, f32[3,256]{1,0:T(4,128)S(1)}, /*index=5*/f32[3,256]{1,0:T(4,128)S(1)}, s32[]{:T(128)}) while((s32[]{:T(128)}, f32[256,3,128]{0,2,1:T(8,128)S(1)}, bf16[9,512,3,128]{1,3,2,0:T(8,128)(2,1)}, ...), condition=%wide.region_7.7_spmd, body=%wide.region_6.6_spmd.sunk | while | flops 101941248 | bytes 2759757 | solution.py:97
  364.1 19.6 %all_to_all.34 = bf16[8,64,384]{2,1,0:T(8,128)(2,1)S(1)} all-to-all(bf16[8,64,384]{2,1,0:T(8,128)(2,1)} %bitcast.111), channel_id=1, replica_groups=mesh['seq'=64,'head'=8] {'head'}, dimensions={0} | all-to-all | bytes 786432 | tf_op jit(solution)/shard_map/all_to_all | solution.py:101
  (115 shorter events, 78.5 us)
Async XLA Ops:
  8.6 57.0 %copy-start.7 = (s32[2,27]{1,0:T(2,128)S(1)}, s32[2,27]{1,0:T(2,128)}, u32[]{:S(2)}) copy-start(s32[2,27]{1,0:T(2,128)} %param.9) | copy-start | bytes 652
  8.6 39.2 %all-to-all-start = ((bf16[8,2,36864]{2,1,0:T(2,128)(2,1)}), bf16[8,2,36864]{2,1,0:T(2,128)(2,1)}, u32[]{:S(2)}, u32[]{:S(2)}) async-start(bf16[8,2,36864]{2,1,0:T(2,128)(2,1)} %reshape.84), calls=%async_computation | async-start | bytes 2359296 | tf_op jit(solution)/shard_map/all_to_all | solution.py:35
  56.8 31.6 %collective-permute-start = (bf16[2,512,384]{2,1,0:T(8,128)(2,1)S(1)}, bf16[2,512,384]{2,1,0:T(8,128)(2,1)}, u32[]{:S(2)}, u32[]{:S(2)}) collective-permute-start(bf16[2,512,384]{2,1,0:T(8,128)(2,1)S(1)} %bitcast.99), channel_id=1, source_target_pairs={{0,72},{8,80},{16,88},{24,96},{32,104},{40,112},{48,120},{56,128},... | collective-permute-start | bytes 2359304 | tf_op jit(solution)/shard_map/ppermute | solution.py:15
  66.0 33.5 %collective-permute-start.1 = (bf16[2,512,384]{2,1,0:T(8,128)(2,1)S(1)}, bf16[2,512,384]{2,1,0:T(8,128)(2,1)S(1)}, u32[]{:S(2)}, u32[]{:S(2)}) collective-permute-start(bf16[2,512,384]{2,1,0:T(8,128)(2,1)S(1)} %bitcast.100), channel_id=1, source_target_pairs={{0,64},{8,72},{16,80},{24,88},{32,96},{40,104},{48,112},{56,120},{... | collective-permute-start | bytes 2359304 | tf_op jit(solution)/shard_map/ppermute | solution.py:15
  72.6 43.8 %collective-permute-start.2 = (bf16[2,512,384]{2,1,0:T(8,128)(2,1)S(1)}, bf16[2,512,384]{2,1,0:T(8,128)(2,1)S(1)}, u32[]{:S(2)}, u32[]{:S(2)}) collective-permute-start(bf16[2,512,384]{2,1,0:T(8,128)(2,1)S(1)} %bitcast.101), channel_id=1, source_target_pairs={{0,56},{8,64},{16,72},{24,80},{32,88},{40,96},{48,104},{56,112},{6... | collective-permute-start | bytes 2359304 | tf_op jit(solution)/shard_map/ppermute | solution.py:15
  79.9 63.1 %collective-permute-start.3 = (bf16[2,512,384]{2,1,0:T(8,128)(2,1)S(1)}, bf16[2,512,384]{2,1,0:T(8,128)(2,1)}, u32[]{:S(2)}, u32[]{:S(2)}) collective-permute-start(bf16[2,512,384]{2,1,0:T(8,128)(2,1)S(1)} %bitcast.102), channel_id=1, source_target_pairs={{0,8},{8,16},{16,24},{24,32},{32,40},{40,48},{48,56},{56,64},{64,7... | collective-permute-start | bytes 2359304 | tf_op jit(solution)/shard_map/ppermute | solution.py:15
  84.4 60.0 %collective-permute-start.4 = (bf16[2,512,384]{2,1,0:T(8,128)(2,1)S(1)}, bf16[2,512,384]{2,1,0:T(8,128)(2,1)}, u32[]{:S(2)}, u32[]{:S(2)}) collective-permute-start(bf16[2,512,384]{2,1,0:T(8,128)(2,1)S(1)} %bitcast.103), channel_id=1, source_target_pairs={{8,0},{16,8},{24,16},{32,24},{40,32},{48,40},{56,48},{64,56},{72,6... | collective-permute-start | bytes 2359304 | tf_op jit(solution)/shard_map/ppermute | solution.py:15
  88.4 57.4 %collective-permute-start.5 = (bf16[2,512,384]{2,1,0:T(8,128)(2,1)S(1)}, bf16[2,512,384]{2,1,0:T(8,128)(2,1)S(1)}, u32[]{:S(2)}, u32[]{:S(2)}) collective-permute-start(bf16[2,512,384]{2,1,0:T(8,128)(2,1)S(1)} %bitcast.104), channel_id=1, source_target_pairs={{56,0},{64,8},{72,16},{80,24},{88,32},{96,40},{104,48},{112,56},{1... | collective-permute-start | bytes 2359304 | tf_op jit(solution)/shard_map/ppermute | solution.py:15
  99.6 95.5 %collective-permute-start.6 = (bf16[2,512,384]{2,1,0:T(8,128)(2,1)S(1)}, bf16[2,512,384]{2,1,0:T(8,128)(2,1)S(1)}, u32[]{:S(2)}, u32[]{:S(2)}) collective-permute-start(bf16[2,512,384]{2,1,0:T(8,128)(2,1)S(1)} %bitcast.105), channel_id=1, source_target_pairs={{64,0},{72,8},{80,16},{88,24},{96,32},{104,40},{112,48},{120,56},{... | collective-permute-start | bytes 2359304 | tf_op jit(solution)/shard_map/ppermute | solution.py:15
  116.5 142.9 %collective-permute-start.7 = (bf16[2,512,384]{2,1,0:T(8,128)(2,1)S(1)}, bf16[2,512,384]{2,1,0:T(8,128)(2,1)S(1)}, u32[]{:S(2)}, u32[]{:S(2)}) collective-permute-start(bf16[2,512,384]{2,1,0:T(8,128)(2,1)S(1)} %bitcast.106), channel_id=1, source_target_pairs={{72,0},{80,8},{88,16},{96,24},{104,32},{112,40},{120,48},{128,56},... | collective-permute-start | bytes 2359304 | tf_op jit(solution)/shard_map/ppermute | solution.py:15
  278.6 1.5 copy-start
  282.3 10.2 %copy-start.2 = (bf16[256,3,128]{2,0,1:T(8,128)(2,1)S(1)}, bf16[256,3,128]{2,0,1:T(8,128)(2,1)}, u32[]{:S(2)}) copy-start(bf16[256,3,128]{2,0,1:T(8,128)(2,1)} %get-tuple-element.357) | copy-start | bytes 589828 | tf_op jit(solution)/shard_map/while
  282.3 10.2 %copy-start.3 = (bf16[512,3,128]{2,0,1:T(8,128)(2,1)S(1)}, bf16[512,3,128]{2,0,1:T(8,128)(2,1)}, u32[]{:S(2)}) copy-start(bf16[512,3,128]{2,0,1:T(8,128)(2,1)} %get-tuple-element.356) | copy-start | bytes 1179652 | tf_op jit(solution)/shard_map/while
  292.8 7.2 %copy-start.6 = (bf16[256,3,128]{2,0,1:T(8,128)(2,1)S(1)}, bf16[256,3,128]{2,0,1:T(8,128)(2,1)}, u32[]{:S(2)}) copy-start(bf16[256,3,128]{2,0,1:T(8,128)(2,1)} %get-tuple-element.360) | copy-start | bytes 589828 | tf_op jit(solution)/shard_map/while
  300.5 20.0 %copy-start.4 = (bf16[2,256,384]{2,1,0:T(8,128)(2,1)S(1)}, bf16[2,256,384]{2,1,0:T(8,128)(2,1)}, u32[]{:S(2)}) copy-start(bf16[2,256,384]{2,1,0:T(8,128)(2,1)} %get-tuple-element.340) | copy-start | bytes 1179652 | tf_op jit(solution)/shard_map/while
  300.5 20.8 %copy-start.1 = (pred[9,512,512]{1,2,0:T(8,128)(4,1)S(1)}, pred[9,512,512]{1,2,0:T(8,128)(4,1)}, u32[]{:S(2)}) copy-start(pred[9,512,512]{1,2,0:T(8,128)(4,1)} %copy-done) | copy-start | bytes 7077892 | tf_op jit(solution)/shard_map/while
  320.6 0.7 copy-start.5
  321.3 1.5 copy-start
  325.0 10.2 %copy-start.2 = (bf16[256,3,128]{2,0,1:T(8,128)(2,1)S(1)}, bf16[256,3,128]{2,0,1:T(8,128)(2,1)}, u32[]{:S(2)}) copy-start(bf16[256,3,128]{2,0,1:T(8,128)(2,1)} %get-tuple-element.357) | copy-start | bytes 589828 | tf_op jit(solution)/shard_map/while
  325.0 10.2 %copy-start.3 = (bf16[512,3,128]{2,0,1:T(8,128)(2,1)S(1)}, bf16[512,3,128]{2,0,1:T(8,128)(2,1)}, u32[]{:S(2)}) copy-start(bf16[512,3,128]{2,0,1:T(8,128)(2,1)} %get-tuple-element.356) | copy-start | bytes 1179652 | tf_op jit(solution)/shard_map/while
  335.5 7.2 %copy-start.6 = (bf16[256,3,128]{2,0,1:T(8,128)(2,1)S(1)}, bf16[256,3,128]{2,0,1:T(8,128)(2,1)}, u32[]{:S(2)}) copy-start(bf16[256,3,128]{2,0,1:T(8,128)(2,1)} %get-tuple-element.360) | copy-start | bytes 589828 | tf_op jit(solution)/shard_map/while
  343.2 20.0 %copy-start.4 = (bf16[2,256,384]{2,1,0:T(8,128)(2,1)S(1)}, bf16[2,256,384]{2,1,0:T(8,128)(2,1)}, u32[]{:S(2)}) copy-start(bf16[2,256,384]{2,1,0:T(8,128)(2,1)} %get-tuple-element.340) | copy-start | bytes 1179652 | tf_op jit(solution)/shard_map/while
  343.2 20.8 %copy-start.1 = (pred[9,512,512]{1,2,0:T(8,128)(4,1)S(1)}, pred[9,512,512]{1,2,0:T(8,128)(4,1)}, u32[]{:S(2)}) copy-start(pred[9,512,512]{1,2,0:T(8,128)(4,1)} %copy-done) | copy-start | bytes 7077892 | tf_op jit(solution)/shard_map/while
  363.3 0.7 copy-start.5
where the time goes:
time: 386 us; the launch traced here: 384 us
  waiting for transfers between devices  194 us (50%)
  matrix products  60.7 us (16%)
  local copies, waits for them, and re-layouts  56.4 us (15%)
  starting transfers between devices  36.3 us (9%)
  blocking collectives  19.6 us (5%)
  other arithmetic  14.9 us (4%)
    ppermute x8, waiting for transfers between devices, from_behind(): return lax.ppermute(block, axis, route)  162 us
    dot_general x18, matrix products, accumulate(): jnp.einsum('hqk,khd->qhd', weights_of(score), vals3, preferred_element_ty...  39.2 us
    all_to_all x1, waiting for transfers between devices, on_device(): local = lax.all_to_all(qkv, 'head', split_axis=2, concat_axis=1, tiled=True)  31.9 us
    ppermute x8, starting transfers between devices, from_behind(): return lax.ppermute(block, axis, route)  29.1 us
    dot_general x2, matrix products, query_block(): jnp.einsum('qhd,pkhd->phqk', part_q, keys_all, preferred_element_type=jnp...  20.3 us
    all_to_all x1, blocking collectives, on_device(): lax.all_to_all(result, 'head', split_axis=0, concat_axis=1, tiled=True)  19.6 us
    unnamed x15, local copies, waits for them, and re-layouts  18.5 us
    reduce_sum x2, other arithmetic, query_block(): jnp.sum(jnp.exp(video_score - largest[None, ..., None]), axis=(0, 3))  14.1 us
  transfers between devices with their start and end apart: 9, of which 6 were waited for; matrix products, arithmetic and copies ran while one was open for 3% of the time, Pallas kernels for 0%

commit v1 on v0

v1 whole, which is shorter than its diff:
```python
import functools
import math

import jax
import jax.numpy as jnp
from jax import lax
from jax.experimental import pallas as pl
from jax.experimental.pallas import tpu as pltpu
from jax.sharding import PartitionSpec as P

HEAD_DIM = 128
GW = 8
CORES = 2
MESH = pl.DeviceIdType.MESH
NEG = -1e30
C2 = math.log2(math.e) / math.sqrt(HEAD_DIM)
F32 = jnp.float32


def kernel(
    grid_rows, nh, hd,
    qkv, text, mask, out,
    q_s, kv_s, text_s, mask_s, bias_s, m_s, l_s, acc_s, osend_s, orecv_s, lsend_s, lrecv_s, ofin_s,
    own_sem, kv_sem, q_sem, text_sem, a2a_send,
    z_send, z_recv, x_send, x_recv, mk_send, mk_recv, o_send, o_recv, ls_send, ls_recv, out_send, out_sem,
):
    s, my = lax.axis_index("seq"), lax.axis_index("head")
    row, col = s // GW, s % GW
    rows = qkv.shape[1]
    total = rows * nh
    tile = total // 2
    width = hd * HEAD_DIM
    quarters = nh // CORES
    part = rows * CORES
    core, hi = my % CORES, my // CORES
    has_q = [None, col > 0, col < GW - 1]
    has_kv = [None, row > 0, row < grid_rows - 1]
    q_dev = [None, (s - 1, my), (s + 1, my)]
    kv_dev = [None, (s - GW, my), (s + GW, my)]
    peers = [(0, (hi * CORES + 1 - core))]
    for r in [d for d in range(1, quarters) if 2 * d != quarters] + [d for d in range(1, quarters) if 2 * d == quarters]:
        for other in range(CORES):
            peers.append((r, ((hi + r) % quarters) * CORES + (core + other) % CORES))
    my_rows = pl.ds(pl.multiple_of(my * rows, rows), rows)

    def lanes(h, i, n=1):
        return pl.ds(pl.multiple_of((h * hd + i) * HEAD_DIM, HEAD_DIM), n * HEAD_DIM)

    def at(i, n=1):
        return pl.ds(i * HEAD_DIM, n * HEAD_DIM)

    def remote(src, dst, ssem, rsem, dev):
        pltpu.make_async_remote_copy(
            src_ref=src, dst_ref=dst, send_sem=ssem, recv_sem=rsem, device_id=dev, device_id_type=MESH
        ).start()

    def wait(ref, sem):
        pltpu.make_async_copy(ref, ref, sem).wait()

    pltpu.make_async_copy(qkv.at[pl.ds(1, 2), :, lanes(my, 0, hd)], kv_s.at[0, :, my_rows, :], own_sem).start()
    for i in range(hd):
        pltpu.make_async_copy(qkv.at[0, :, lanes(my, i)], q_s.at[0, my_rows, at(i)], q_sem.at[i]).start()
    pltpu.make_async_copy(text, text_s, text_sem).start()

    barrier = pltpu.get_barrier_semaphore()
    count = len(peers)
    for _, p in peers:
        pl.semaphore_signal(barrier, inc=1, device_id=(s, p), device_id_type=MESH)
    for has, dev in zip(has_q[1:] + has_kv[1:], q_dev[1:] + kv_dev[1:]):
        count = count + has.astype(jnp.int32)

        @pl.when(has)
        def _():
            pl.semaphore_signal(barrier, inc=1, device_id=dev, device_id_type=MESH)

    mask_s[0] = jnp.zeros_like(mask_s[0])
    mask_s[0, 0:2, 0:27] = mask[...]
    pl.semaphore_wait(barrier, count)

    def send_kv(i, n, r):
        p = peers[0][1] if r is None else r[1]
        rsem = own_sem if r is None else kv_sem.at[i, (quarters - r[0]) % quarters]
        remote(
            qkv.at[pl.ds(1, 2), :, lanes(p, i, n)], kv_s.at[0, :, my_rows, at(i, n)], a2a_send, rsem, (s, p)
        )

    def send_q(i, p):
        remote(qkv.at[0, :, lanes(p, i)], q_s.at[0, my_rows, at(i)], a2a_send, q_sem.at[i], (s, p))

    send_kv(0, hd, None)
    for r in peers[1:]:
        send_kv(0, 1, r)
    for k in (1, 2):
        @pl.when(has_q[k])
        def _():
            remote(mask_s.at[0], mask_s.at[3 - k], mk_send.at[k - 1], mk_recv.at[2 - k], q_dev[k])

    def forward_kv(i, g):
        where = pl.ds(pl.multiple_of(g * part, part), part)
        for k in (1, 2):
            @pl.when(has_kv[k])
            def _():
                ref = kv_s.at[0, :, where, at(i)]
                remote(ref, kv_s.at[3 - k, :, where, at(i)], z_send.at[k - 1], z_recv.at[i, 2 - k], kv_dev[k])

    own_part = pl.ds(pl.multiple_of(hi * part, part), part)
    wait(kv_s.at[0, :, own_part, :], own_sem)
    for i in range(hd):
        forward_kv(i, hi)
    for i in range(hd):
        if i > 0:
            for r in peers[1:]:
                send_kv(i, 1, r)
        for _, p in peers:
            send_q(i, p)

    m_s[...] = jnp.full_like(m_s, NEG)
    l_s[...] = jnp.zeros_like(l_s)
    acc_s[...] = jnp.zeros_like(acc_s)

    def update(i, qs, k, v, biases):
        q = q_s[qs, :, at(i)]
        m_old = m_s[qs, i]
        scores = []
        m_new = m_old
        for f, b in enumerate(biases):
            sc = lax.dot_general(
                k[f * tile:(f + 1) * tile], q, (((1,), (1,)), ((), ())), preferred_element_type=F32
            )
            top = jnp.max(sc, axis=0, keepdims=True)
            m_new = jnp.maximum(m_new, top if b is None else top + b)
            scores.append(sc)
        alpha = jnp.exp2((m_old - m_new) * C2)
        big = m_new * C2
        l_new = l_s[qs, i] * alpha
        acc = acc_s[qs, i] * alpha
        for f, b in enumerate(biases):
            sub = big if b is None else jnp.where(b < 0, -NEG, big)
            e = jnp.exp2(scores[f] * C2 - sub)
            l_new = l_new + jnp.sum(e, axis=0, keepdims=True)
            acc = acc + lax.dot_general(
                v[f * tile:(f + 1) * tile], e.astype(jnp.bfloat16), (((0,), (0,)), ((), ())),
                preferred_element_type=F32,
            )
        m_s[qs, i] = m_new
        l_s[qs, i] = l_new
        acc_s[qs, i] = acc

    def update_kv(i, qs, ks):
        update(i, qs, kv_s[ks, 0, :, at(i)], kv_s[ks, 1, :, at(i)], [bias_s[qs, ks, 0], bias_s[qs, ks, 1]])

    def make_bias(qs):
        lane = lax.broadcasted_iota(jnp.int32, (1, total), 1)
        for ks in range(3):
            for kf in range(2):
                picked = []
                for qf in range(2):
                    o = (kf - qf + 1) * 9 + (1, 0, 2)[ks] * 3 + (1, 2, 0)[qs]
                    picked.append(jnp.broadcast_to(mask_s[qs, qf:qf + 1, o:o + 1], (1, total)))
                chosen = jnp.where(lane < tile, picked[0], picked[1])
                bias_s[qs, ks, kf] = jnp.where(chosen > 0, 0.0, NEG).astype(F32)

    make_bias(0)
    wait(text_s, text_sem)
    for i in range(hd):
        for r in dict.fromkeys(r for r, _ in peers[1:]):
            back = (quarters - r) % quarters
            g = (hi + back) % quarters
            where = pl.ds(pl.multiple_of(g * part, part), part)
            wait(kv_s.at[0, :, where, at(i)], kv_sem.at[i, back])
            forward_kv(i, g)
        wait(q_s.at[0, :, at(i)], q_sem.at[i])
        for k in (1, 2):
            @pl.when(has_q[k])
            def _():
                remote(q_s.at[0, :, at(i)], q_s.at[3 - k, :, at(i)], x_send.at[k - 1], x_recv.at[i, 2 - k], q_dev[k])
        update(i, 0, text_s[0, :, at(i)], text_s[1, :, at(i)], [None] * (text_s.shape[1] // tile))
        update_kv(i, 0, 0)

    for k in (1, 2):
        @pl.when(has_q[k])
        def _():
            wait(mask_s.at[k], mk_recv.at[k - 1])
            make_bias(k)

        @pl.when(jnp.logical_not(has_q[k]))
        def _():
            orecv_s[k - 1] = jnp.zeros_like(orecv_s[k - 1])
            lrecv_s[k - 1] = jnp.full_like(lrecv_s[k - 1], NEG)
    for i in range(hd):
        for k in (1, 2):
            @pl.when(has_q[k])
            def _():
                wait(q_s.at[k, :, at(i)], x_recv.at[i, k - 1])
                update_kv(i, k, 0)

    def finish(i):
        parts = []
        for k in (1, 2):
            @pl.when(has_q[k])
            def _():
                wait(orecv_s.at[k - 1, i], o_recv.at[i, k - 1])
                wait(lrecv_s.at[k - 1, i], ls_recv.at[i, k - 1])

            parts.append((lrecv_s[k - 1, i, 0:1], orecv_s[k - 1, i].astype(F32)))
        l = l_s[0, i]
        lse = m_s[0, i] * C2 + jnp.log2(l)
        top = jnp.maximum(lse, jnp.maximum(parts[0][0], parts[1][0]))
        w = jnp.exp2(lse - top)
        w1, w2 = jnp.exp2(parts[0][0] - top), jnp.exp2(parts[1][0] - top)
        scale = 1.0 / (w + w1 + w2)
        o = acc_s[0, i] * (w * scale / l) + parts[0][1] * (w1 * scale) + parts[1][1] * (w2 * scale)
        ofin_s[:, at(i)] = o.T.astype(jnp.bfloat16)
        for _, p in peers:
            remote(
                ofin_s.at[pl.ds(pl.multiple_of(p * rows, rows), rows), at(i)], out.at[:, lanes(my, i)],
                out_send, out_sem, (s, p),
            )
        pltpu.make_async_copy(ofin_s.at[my_rows, at(i)], out.at[:, lanes(my, i)], out_sem).start()

    for i in range(hd):
        for k in (1, 2):
            @pl.when(has_kv[k])
            def _():
                wait(kv_s.at[k, :, :, at(i)], z_recv.at[i, k - 1])
                for qs in (1, 2, 0):
                    if qs == 0:
                        update_kv(i, 0, k)
                    else:
                        @pl.when(has_q[qs])
                        def _():
                            update_kv(i, qs, k)

        for k in (1, 2):
            @pl.when(has_q[k])
            def _():
                l = l_s[k, i]
                some = l > 0
                osend_s[k - 1, i] = (acc_s[k, i] * jnp.where(some, 1.0 / l, 0.0)).astype(jnp.bfloat16)
                lsend_s[k - 1, i] = jnp.broadcast_to(
                    jnp.where(some, m_s[k, i] * C2 + jnp.log2(l), NEG), lsend_s.shape[2:]
                )
                remote(osend_s.at[k - 1, i], orecv_s.at[2 - k, i], o_send.at[k - 1], o_recv.at[i, 2 - k], q_dev[k])
                remote(lsend_s.at[k - 1, i], lrecv_s.at[2 - k, i], ls_send.at[k - 1], ls_recv.at[i, 2 - k], q_dev[k])
        if i > 0:
            finish(i - 1)
    finish(hd - 1)

    less = total - rows
    wait(kv_s.at[0, :, pl.ds(0, less), :], a2a_send)
    wait(q_s.at[0, pl.ds(0, less), :], a2a_send)
    for k in (1, 2):
        @pl.when(has_kv[k])
        def _():
            wait(kv_s.at[0], z_send.at[k - 1])

        @pl.when(has_q[k])
        def _():
            wait(q_s.at[0], x_send.at[k - 1])
            wait(mask_s.at[0], mk_send.at[k - 1])
            wait(osend_s.at[k - 1], o_send.at[k - 1])
            wait(lsend_s.at[k - 1], ls_send.at[k - 1])
    wait(ofin_s.at[pl.ds(0, less), :], out_send)
    wait(out, out_sem)


def solution(mesh):
    nh = mesh.shape["head"]
    grid_rows = mesh.shape["seq"] // GW

    def on_device(qkv, text_kv, window_mask):
        _, rows, d = qkv.shape
        txt, width = text_kv.shape[1:]
        hd = width // HEAD_DIM
        total = rows * nh
        quarters = nh // CORES
        bf = jnp.bfloat16
        dma = pltpu.SemaphoreType.DMA
        return pl.pallas_call(
            functools.partial(kernel, grid_rows, nh, hd),
            out_shape=jax.ShapeDtypeStruct((rows, d), bf),
            in_specs=[
                pl.BlockSpec(memory_space=pl.ANY),
                pl.BlockSpec(memory_space=pl.ANY),
                pl.BlockSpec(memory_space=pltpu.VMEM),
            ],
            out_specs=pl.BlockSpec(memory_space=pltpu.VMEM),
            scratch_shapes=[
                pltpu.VMEM((3, total, width), bf),
                pltpu.VMEM((3, 2, total, width), bf),
                pltpu.VMEM((2, txt, width), bf),
                pltpu.VMEM((3, 8, 128), jnp.int32),
                pltpu.VMEM((3, 3, 2, 1, total), F32),
                pltpu.VMEM((3, hd, 1, total), F32),
                pltpu.VMEM((3, hd, 1, total), F32),
                pltpu.VMEM((3, hd, HEAD_DIM, total), F32),
                pltpu.VMEM((2, hd, HEAD_DIM, total), bf),
                pltpu.VMEM((2, hd, HEAD_DIM, total), bf),
                pltpu.VMEM((2, hd, 8, total), F32),
                pltpu.VMEM((2, hd, 8, total), F32),
                pltpu.VMEM((total, width), bf),
                dma, dma((hd, quarters)), dma((hd,)), dma, dma,
                dma((2,)), dma((hd, 2)), dma((2,)), dma((hd, 2)), dma((2,)), dma((2,)),
                dma((2,)), dma((hd, 2)), dma((2,)), dma((hd, 2)), dma, dma,
            ],
            compiler_params=pltpu.CompilerParams(
                collective_id=0, has_side_effects=True, vmem_limit_bytes=48 << 20
            ),
            cost_estimate=pl.CostEstimate(
                flops=4 * total * hd * HEAD_DIM * (9 * total + txt),
                bytes_accessed=8 * rows * d,
                transcendentals=total * hd * (9 * total + txt),
            ),
        )(qkv, text_kv, window_mask)

    return jax.shard_map(
        on_device, mesh=mesh,
        in_specs=(P(None, ("seq", "head"), None), P(None, None, "head"), P("seq", None)),
        out_specs=P(("seq", "head"), None), check_vma=False,
    )
```

time: 386 us -> 95.5 us (0.25)
  the two profiles are of different devices: /device:TPU:6 before, /device:TPU:73 now
where the time goes in v1:
time: 95.5 us; the launch traced here: 95.3 us
  Pallas kernels  91.5 us (96%)
  local copies, waits for them, and re-layouts  3.69 us (4%)
    pallas_call x1, Pallas kernels, on_device(): pl.pallas_call(functools.partial(kernel, grid_rows, nh, hd), out_shape=ja...  91.5 us
    unnamed x7, local copies, waits for them, and re-layouts  3.69 us

profile of v1, /device:TPU:73, one launch (start us, length us, event | category | flops | bytes accessed | tf_op | source)
XLA Modules:
  0.0 95.3 jit_solution(12052746132869917913)
XLA Ops:
  0.0 0.0 copy-start
  0.0 1.3 %copy-done = bf16[3,64,3072]{2,1,0:T(8,128)(2,1)S(1)} copy-done((bf16[3,64,3072]{2,1,0:T(8,128)(2,1)S(1)}, bf16[3,64,3072]{2,1,0:T(8,128)(2,1)}, u32[]{:S(2)}) %copy-start) | copy-done | bytes 1179672
  1.3 0.0 copy-start.1
  1.3 1.0 %copy-done.1 = bf16[2,256,384]{2,1,0:T(8,128)(2,1)S(1)} copy-done((bf16[2,256,384]{2,1,0:T(8,128)(2,1)S(1)}, bf16[2,256,384]{2,1,0:T(8,128)(2,1)}, u32[]{:S(2)}) %copy-start.1) | copy-done | bytes 393240
  2.3 0.0 copy-start.2
  2.3 0.7 copy-done.2
  2.9 91.5 %shard_map.37 = bf16[64,3072]{1,0:T(8,128)(2,1)S(1)} custom-call(bf16[3,64,3072]{2,1,0:T(8,128)(2,1)S(1)} %copy-done, bf16[2,256,384]{2,1,0:T(8,128)(2,1)S(1)} %copy-done.1, s32[2,27]{1,0:T(2,128)S(1)} %copy-done.2), custom_call_target="tpu_custom_call" | custom-call | flops 3825205248 | bytes 1572864 | tf_op jit(solution)/shard_map/pallas_call | solution.py:279
  94.5 0.7 copy.5
Async XLA Ops:
  0.0 1.3 %copy-start = (bf16[3,64,3072]{2,1,0:T(8,128)(2,1)S(1)}, bf16[3,64,3072]{2,1,0:T(8,128)(2,1)}, u32[]{:S(2)}) copy-start(bf16[3,64,3072]{2,1,0:T(8,128)(2,1)} %qkv.1) | copy-start | bytes 3538948
  1.3 1.0 %copy-start.1 = (bf16[2,256,384]{2,1,0:T(8,128)(2,1)S(1)}, bf16[2,256,384]{2,1,0:T(8,128)(2,1)}, u32[]{:S(2)}) copy-start(bf16[2,256,384]{2,1,0:T(8,128)(2,1)} %text.1) | copy-start | bytes 1179652
  2.3 0.7 copy-start.2

commit v2 on v1

v2 whole, which is shorter than its diff:
```python
import functools
import math

import jax
import jax.numpy as jnp
from jax import lax
from jax.experimental import pallas as pl
from jax.experimental.pallas import tpu as pltpu
from jax.sharding import PartitionSpec as P

HEAD_DIM = 128
GW = 8
CORES = 2
MESH = pl.DeviceIdType.MESH
NEG = -1e30
C2 = math.log2(math.e) / math.sqrt(HEAD_DIM)
F32 = jnp.float32
MODES = (0, 0, 1)
PLAN = (
    ("y", "kv", 0), ("f", 0, 0), ("ys", "kv", 0), ("y", "q", 0), ("f", 0, 1), ("f", 0, 3), ("f", 0, 2),
    ("ys", "q", 0), ("y", "q", 2), ("q", 0), ("text", 0), ("c", 0, 0, 0), ("ys", "q", 2), ("y", "kv", 1),
    ("c", 0, 1, 0), ("c", 0, 2, 0), ("fs", 0), ("q", 2), ("qs", 2), ("ys", "kv", 1), ("y", "kv", 2), ("f", 1, 0),
    ("f", 1, 1), ("f", 1, 3), ("f", 1, 2), ("c", 0, 1, 1), ("c", 0, 1, 2), ("c", 0, 2, 1), ("c", 0, 2, 2), ("r", 0),
    ("c", 0, 0, 1), ("c", 0, 0, 2), ("text", 2), ("ys", "kv", 2), ("y", "q", 1), ("n", 0), ("f", 2, 0), ("f", 2, 1),
    ("f", 2, 3), ("f", 2, 2), ("c", 2, 0, 0), ("c", 2, 1, 0), ("c", 2, 2, 0), ("q", 1), ("text", 1), ("c", 1, 0, 0),
    ("c", 1, 1, 0), ("c", 1, 2, 0), ("c", 2, 1, 1), ("c", 2, 1, 2), ("c", 2, 2, 1), ("c", 2, 2, 2), ("r", 2),
    ("c", 2, 0, 1), ("c", 2, 0, 2), ("c", 1, 1, 1), ("c", 1, 1, 2), ("c", 1, 2, 1), ("c", 1, 2, 2), ("r", 1),
    ("c", 1, 0, 1), ("c", 1, 0, 2), ("n", 2), ("n", 1),
)


def kernel(
    grid_rows, nh, hd,
    qkv, text, mask, out,
    q_s, kv_s, text_s, mask_s, bias_s, m_s, l_s, acc_s, osend_s, orecv_s, lsend_s, lrecv_s, ofin_s,
    own_sem, kv_sem, q_sem, text_sem, a2a_send,
    kv_send, kv_recv, q_send, q_recv, mk_send, mk_recv, o_send, o_recv, ls_send, ls_recv, out_send, out_sem,
):
    s, my = lax.axis_index("seq"), lax.axis_index("head")
    row, col = s // GW, s % GW
    rows = qkv.shape[1]
    total = rows * nh
    tile = total // 2
    quarters = nh // CORES
    part = rows * CORES
    core, hi = my % CORES, my // CORES
    has = [[None, row > 0, row < grid_rows - 1], [None, col > 0, col < GW - 1]]
    dev = [[None, (s - GW, my), (s + GW, my)], [None, (s - 1, my), (s + 1, my)]]
    kv_axis = [MODES[i] for i in range(hd)]
    q_axis = [1 - MODES[i] for i in range(hd)]
    mate = hi * CORES + 1 - core
    far = [(r, ((hi + r) % quarters) * CORES + (core + o) % CORES) for r in range(1, quarters) for o in range(CORES)]
    peers = [(0, mate)] + sorted(far, key=lambda p: 2 * p[0] == quarters)
    my_rows = pl.ds(pl.multiple_of(my * rows, rows), rows)

    def lanes(h, i, n=1):
        return pl.ds(pl.multiple_of((h * hd + i) * HEAD_DIM, HEAD_DIM), n * HEAD_DIM)

    def at(i, n=1):
        return pl.ds(i * HEAD_DIM, n * HEAD_DIM)

    def remote(src, dst, ssem, rsem, device):
        pltpu.make_async_remote_copy(
            src_ref=src, dst_ref=dst, send_sem=ssem, recv_sem=rsem, device_id=device, device_id_type=MESH
        ).start()

    def wait(ref, sem):
        pltpu.make_async_copy(ref, ref, sem).wait()

    pltpu.make_async_copy(qkv.at[pl.ds(1, 2), :, lanes(my, 0, hd)], kv_s.at[0, :, my_rows, :], own_sem).start()
    for i in range(hd):
        pltpu.make_async_copy(qkv.at[0, :, lanes(my, i)], q_s.at[0, my_rows, at(i)], q_sem.at[i]).start()
    pltpu.make_async_copy(text, text_s, text_sem).start()

    barrier = pltpu.get_barrier_semaphore()
    count = len(peers)
    for _, p in peers:
        pl.semaphore_signal(barrier, inc=1, device_id=(s, p), device_id_type=MESH)
    for a in (0, 1):
        for k in (1, 2):
            count = count + has[a][k].astype(jnp.int32)

            @pl.when(has[a][k])
            def _():
                pl.semaphore_signal(barrier, inc=1, device_id=dev[a][k], device_id_type=MESH)

    m_s[...] = jnp.full_like(m_s, NEG)
    l_s[...] = jnp.zeros_like(l_s)
    acc_s[...] = jnp.zeros_like(acc_s)
    pl.semaphore_wait(barrier, count)

    remote(qkv.at[pl.ds(1, 2), :, lanes(mate, 0, hd)], kv_s.at[0, :, my_rows, :], a2a_send.at[2, 0], own_sem, (s, mate))

    def send(kind, i):
        for r, p in peers:
            if kind == 0:
                remote(qkv.at[0, :, lanes(p, i)], q_s.at[0, my_rows, at(i)], a2a_send.at[0, i], q_sem.at[i], (s, p))
            elif r > 0:
                remote(
                    qkv.at[pl.ds(1, 2), :, lanes(p, i)], kv_s.at[0, :, my_rows, at(i)],
                    a2a_send.at[1, i], kv_sem.at[i, quarters - r], (s, p),
                )

    def sent(kind, i):
        if kind == 0:
            wait(q_s.at[0, pl.ds(0, total - rows), at(i)], a2a_send.at[0, i])
        else:
            wait(kv_s.at[0, :, pl.ds(0, total - part), at(i)], a2a_send.at[1, i])

    def make_bias(mode, qs):
        which = 0 if qs == 0 else 1 + 2 * (1 - mode) + qs - 1
        lane = lax.broadcasted_iota(jnp.int32, (1, total), 1)
        for ks in range(3):
            for kf in range(2):
                picked = []
                for qf in range(2):
                    along_kv, along_q = (1, 0, 2)[ks], (1, 2, 0)[qs]
                    o = (kf - qf + 1) * 9 + (along_kv * 3 + along_q if mode == 0 else along_q * 3 + along_kv)
                    picked.append(jnp.broadcast_to(mask_s[which, qf:qf + 1, o:o + 1], (1, total)))
                chosen = jnp.where(lane < tile, picked[0], picked[1])
                bias_s[mode, qs, ks, kf] = jnp.where(chosen > 0, 0.0, NEG).astype(F32)

    def forward_kv(i, back):
        g = (hi + back) % quarters
        where = pl.ds(pl.multiple_of(g * part, part), part)
        if back > 0:
            wait(kv_s.at[0, :, where, at(i)], kv_sem.at[i, back])
        a = kv_axis[i]
        for k in (1, 2):
            @pl.when(has[a][k])
            def _():
                remote(
                    kv_s.at[0, :, where, at(i)], kv_s.at[3 - k, :, where, at(i)],
                    kv_send.at[i, k - 1], kv_recv.at[i, 2 - k], dev[a][k],
                )

    def forwarded_kv(i):
        for k in (1, 2):
            @pl.when(has[kv_axis[i]][k])
            def _():
                wait(kv_s.at[0, :, :, at(i)], kv_send.at[i, k - 1])

    def forward_q(i):
        wait(q_s.at[0, :, at(i)], q_sem.at[i])
        a = q_axis[i]
        for k in (1, 2):
            @pl.when(has[a][k])
            def _():
                remote(q_s.at[0, :, at(i)], q_s.at[3 - k, :, at(i)], q_send.at[i, k - 1], q_recv.at[i, 2 - k], dev[a][k])

    def forwarded_q(i):
        for k in (1, 2):
            @pl.when(has[q_axis[i]][k])
            def _():
                wait(q_s.at[0, :, at(i)], q_send.at[i, k - 1])

    def update(i, qs, k, v, biases):
        q = q_s[qs, :, at(i)]
        m_old = m_s[qs, i]
        scores = []
        m_new = m_old
        for f, b in enumerate(biases):
            sc = lax.dot_general(
                k[f * tile:(f + 1) * tile], q, (((1,), (1,)), ((), ())), preferred_element_type=F32
            )
            top = jnp.max(sc, axis=0, keepdims=True)
            m_new = jnp.maximum(m_new, top if b is None else top + b)
            scores.append(sc)
        alpha = jnp.exp2((m_old - m_new) * C2)
        big = m_new * C2
        l_new = l_s[qs, i] * alpha
        acc = acc_s[qs, i] * alpha
        for f, b in enumerate(biases):
            sub = big if b is None else jnp.where(b < 0, -NEG, big)
            e = jnp.exp2(scores[f] * C2 - sub)
            l_new = l_new + jnp.sum(e, axis=0, keepdims=True)
            acc = acc + lax.dot_general(
                v[f * tile:(f + 1) * tile], e.astype(jnp.bfloat16), (((0,), (0,)), ((), ())),
                preferred_element_type=F32,
            )
        m_s[qs, i] = m_new
        l_s[qs, i] = l_new
        acc_s[qs, i] = acc

    landed = set()

    def block(i, qs, ks):
        need_q, need_kv = qs and ("q", i, qs) not in landed, ks and ("kv", i, ks) not in landed
        if need_q:
            landed.add(("q", i, qs))

            @pl.when(has[q_axis[i]][qs])
            def _():
                wait(q_s.at[qs, :, at(i)], q_recv.at[i, qs - 1])
        if need_kv:
            landed.add(("kv", i, ks))

            @pl.when(has[kv_axis[i]][ks])
            def _():
                wait(kv_s.at[ks, :, :, at(i)], kv_recv.at[i, ks - 1])

        def go():
            update(
                i, qs, kv_s[ks, 0, :, at(i)], kv_s[ks, 1, :, at(i)],
                [bias_s[MODES[i], qs, ks, 0], bias_s[MODES[i], qs, ks, 1]],
            )

        guards = ([has[q_axis[i]][qs]] if qs else []) + ([has[kv_axis[i]][ks]] if ks else [])
        if guards:
            pl.when(functools.reduce(jnp.logical_and, guards))(go)
        else:
            go()

    def text_block(i):
        update(i, 0, text_s[0, :, at(i)], text_s[1, :, at(i)], [None] * (text_s.shape[1] // tile))

    def give_back(i):
        a = q_axis[i]
        for k in (1, 2):
            @pl.when(has[a][k])
            def _():
                l = l_s[k, i]
                some = l > 0
                osend_s[k - 1, i] = (acc_s[k, i] * jnp.where(some, 1.0 / l, 0.0)).astype(jnp.bfloat16)
                lsend_s[k - 1, i] = jnp.broadcast_to(
                    jnp.where(some, m_s[k, i] * C2 + jnp.log2(l), NEG), lsend_s.shape[2:]
                )
                remote(osend_s.at[k - 1, i], orecv_s.at[2 - k, i], o_send.at[i, k - 1], o_recv.at[i, 2 - k], dev[a][k])
                remote(lsend_s.at[k - 1, i], lrecv_s.at[2 - k, i], ls_send.at[i, k - 1], ls_recv.at[i, 2 - k], dev[a][k])

    def finish(i):
        a = q_axis[i]
        parts = []
        for k in (1, 2):
            @pl.when(has[a][k])
            def _():
                wait(orecv_s.at[k - 1, i], o_recv.at[i, k - 1])
                wait(lrecv_s.at[k - 1, i], ls_recv.at[i, k - 1])

            @pl.when(jnp.logical_not(has[a][k]))
            def _():
                orecv_s[k - 1, i] = jnp.zeros_like(orecv_s[k - 1, i])
                lrecv_s[k - 1, i] = jnp.full_like(lrecv_s[k - 1, i], NEG)

            parts.append((lrecv_s[k - 1, i, 0:1], orecv_s[k - 1, i].astype(F32)))
        l = l_s[0, i]
        lse = m_s[0, i] * C2 + jnp.log2(l)
        top = jnp.maximum(lse, jnp.maximum(parts[0][0], parts[1][0]))
        w = jnp.exp2(lse - top)
        w1, w2 = jnp.exp2(parts[0][0] - top), jnp.exp2(parts[1][0] - top)
        scale = 1.0 / (w + w1 + w2)
        o = acc_s[0, i] * (w * scale / l) + parts[0][1] * (w1 * scale) + parts[1][1] * (w2 * scale)
        ofin_s[:, at(i)] = o.T.astype(jnp.bfloat16)
        for _, p in peers:
            remote(
                ofin_s.at[pl.ds(pl.multiple_of(p * rows, rows), rows), at(i)], out.at[:, lanes(my, i)],
                out_send, out_sem, (s, p),
            )
        pltpu.make_async_copy(ofin_s.at[my_rows, at(i)], out.at[:, lanes(my, i)], out_sem).start()

    def masks():
        mask_s[0] = jnp.zeros_like(mask_s[0])
        mask_s[0, 0:2, 0:27] = mask[...]
        for a in (0, 1):
            for k in (1, 2):
                @pl.when(has[a][k])
                def _():
                    remote(
                        mask_s.at[0], mask_s.at[1 + 2 * a + 2 - k], mk_send.at[a, k - 1], mk_recv.at[a, 2 - k], dev[a][k]
                    )

    def biases():
        for mode in sorted(set(MODES)):
            make_bias(mode, 0)
            for k in (1, 2):
                @pl.when(has[1 - mode][k])
                def _():
                    wait(mask_s.at[1 + 2 * (1 - mode) + k - 1], mk_recv.at[1 - mode, k - 1])
                    make_bias(mode, k)

    first = True
    kinds = {"q": 0, "kv": 1}
    for op, *rest in PLAN:
        if op == "y":
            send(kinds[rest[0]], rest[1])
        elif op == "ys":
            sent(kinds[rest[0]], rest[1])
        elif op == "f":
            if first:
                first = False
                own_part = pl.ds(pl.multiple_of(hi * part, part), part)
                wait(kv_s.at[0, :, own_part, :], own_sem)
                forward_kv(*rest)
                masks()
                biases()
                wait(text_s, text_sem)
            else:
                forward_kv(*rest)
        elif op == "fs":
            forwarded_kv(rest[0])
        elif op == "q":
            forward_q(rest[0])
        elif op == "qs":
            forwarded_q(rest[0])
        elif op == "text":
            text_block(rest[0])
        elif op == "c":
            block(*rest)
        elif op == "r":
            give_back(rest[0])
        elif op == "n":
            finish(rest[0])

    wait(kv_s.at[0, :, pl.ds(0, rows), :], a2a_send.at[2, 0])
    for i in range(hd):
        for kind, name in ((0, "q"), (1, "kv")):
            if ("ys", name, i) not in PLAN:
                sent(kind, i)
        if ("fs", i) not in PLAN:
            forwarded_kv(i)
        if ("qs", i) not in PLAN:
            forwarded_q(i)
        for k in (1, 2):
            @pl.when(has[q_axis[i]][k])
            def _():
                wait(osend_s.at[k - 1, i], o_send.at[i, k - 1])
                wait(lsend_s.at[k - 1, i], ls_send.at[i, k - 1])
    for a in (0, 1):
        for k in (1, 2):
            @pl.when(has[a][k])
            def _():
                wait(mask_s.at[0], mk_send.at[a, k - 1])
                if 1 - a not in MODES:
                    wait(mask_s.at[1 + 2 * a + k - 1], mk_recv.at[a, k - 1])
    wait(ofin_s.at[pl.ds(0, total - rows), :], out_send)
    wait(out, out_sem)


def solution(mesh):
    nh = mesh.shape["head"]
    grid_rows = mesh.shape["seq"] // GW

    def on_device(qkv, text_kv, window_mask):
        _, rows, d = qkv.shape
        txt, width = text_kv.shape[1:]
        hd = width // HEAD_DIM
        total = rows * nh
        quarters = nh // CORES
        bf = jnp.bfloat16
        dma = pltpu.SemaphoreType.DMA
        return pl.pallas_call(
            functools.partial(kernel, grid_rows, nh, hd),
            out_shape=jax.ShapeDtypeStruct((rows, d), bf),
            in_specs=[
                pl.BlockSpec(memory_space=pl.ANY),
                pl.BlockSpec(memory_space=pl.ANY),
                pl.BlockSpec(memory_space=pltpu.VMEM),
            ],
            out_specs=pl.BlockSpec(memory_space=pltpu.VMEM),
            scratch_shapes=[
                pltpu.VMEM((3, total, width), bf),
                pltpu.VMEM((3, 2, total, width), bf),
                pltpu.VMEM((2, txt, width), bf),
                pltpu.VMEM((5, 8, 128), jnp.int32),
                pltpu.VMEM((2, 3, 3, 2, 1, total), F32),
                pltpu.VMEM((3, hd, 1, total), F32),
                pltpu.VMEM((3, hd, 1, total), F32),
                pltpu.VMEM((3, hd, HEAD_DIM, total), F32),
                pltpu.VMEM((2, hd, HEAD_DIM, total), bf),
                pltpu.VMEM((2, hd, HEAD_DIM, total), bf),
                pltpu.VMEM((2, hd, 8, total), F32),
                pltpu.VMEM((2, hd, 8, total), F32),
                pltpu.VMEM((total, width), bf),
                dma, dma((hd, quarters)), dma((hd,)), dma, dma((3, hd)),
                dma((hd, 2)), dma((hd, 2)), dma((hd, 2)), dma((hd, 2)), dma((2, 2)), dma((2, 2)),
                dma((hd, 2)), dma((hd, 2)), dma((hd, 2)), dma((hd, 2)), dma, dma,
            ],
            compiler_params=pltpu.CompilerParams(
                collective_id=0, has_side_effects=True, vmem_limit_bytes=60 << 20
            ),
            cost_estimate=pl.CostEstimate(
                flops=4 * total * hd * HEAD_DIM * (9 * total + txt),
                bytes_accessed=8 * rows * d,
                transcendentals=total * hd * (9 * total + txt),
            ),
        )(qkv, text_kv, window_mask)

    return jax.shard_map(
        on_device, mesh=mesh,
        in_specs=(P(None, ("seq", "head"), None), P(None, None, "head"), P("seq", None)),
        out_specs=P(("seq", "head"), None), check_vma=False,
    )
```

time: 95.5 us -> 101 us (1.058)
  the two profiles are of different devices: /device:TPU:73 before, /device:TPU:15 now
where the time goes in v2:
time: 101 us
  Pallas kernels  99.5 us (99%)
  local copies, waits for them, and re-layouts  1.77 us (2%)
    pallas_call x1, Pallas kernels, on_device(): pl.pallas_call(functools.partial(kernel, grid_rows, nh, hd), out_shape=ja...  99.5 us

profile of v2, /device:TPU:15, one launch (start us, length us, event | category | flops | bytes accessed | tf_op | source)
XLA Modules:
  0.0 101.3 jit_solution(13838984850395549523)
XLA Ops:
  0.0 99.5 %shard_map.37 = bf16[64,3072]{1,0:T(8,128)(2,1)} custom-call(bf16[3,64,3072]{2,1,0:T(8,128)(2,1)} %qkv.1, bf16[2,256,384]{2,1,0:T(8,128)(2,1)} %text.1, s32[2,27]{1,0:T(2,128)} %mask.1), custom_call_target="tpu_custom_call" | custom-call | flops 3825205248 | bytes 1572864 | tf_op jit(solution)/shard_map/pallas_call | solution.py:351
  99.5 1.8 %copy.5 = bf16[64,3072]{1,0:T(8,128)(2,1)} copy(bf16[64,3072]{1,0:T(8,128)(2,1)} %shard_map.37) | data formatting | bytes 786432

commit v3 on v2

--- a/solution.py
+++ b/solution.py
@@ -15,42 +15,61 @@
 NEG = -1e30
 C2 = math.log2(math.e) / math.sqrt(HEAD_DIM)
 F32 = jnp.float32
-MODES = (0, 0, 1)
+MODES = (0, 0, 0)
+EDGE = GW // 2 - 1
+ROUTES = {1: (0, 7)}
 PLAN = (
-    ("y", "kv", 0), ("f", 0, 0), ("ys", "kv", 0), ("y", "q", 0), ("f", 0, 1), ("f", 0, 3), ("f", 0, 2),
-    ("ys", "q", 0), ("y", "q", 2), ("q", 0), ("text", 0), ("c", 0, 0, 0), ("ys", "q", 2), ("y", "kv", 1),
-    ("c", 0, 1, 0), ("c", 0, 2, 0), ("fs", 0), ("q", 2), ("qs", 2), ("ys", "kv", 1), ("y", "kv", 2), ("f", 1, 0),
-    ("f", 1, 1), ("f", 1, 3), ("f", 1, 2), ("c", 0, 1, 1), ("c", 0, 1, 2), ("c", 0, 2, 1), ("c", 0, 2, 2), ("r", 0),
-    ("c", 0, 0, 1), ("c", 0, 0, 2), ("text", 2), ("ys", "kv", 2), ("y", "q", 1), ("n", 0), ("f", 2, 0), ("f", 2, 1),
-    ("f", 2, 3), ("f", 2, 2), ("c", 2, 0, 0), ("c", 2, 1, 0), ("c", 2, 2, 0), ("q", 1), ("text", 1), ("c", 1, 0, 0),
-    ("c", 1, 1, 0), ("c", 1, 2, 0), ("c", 2, 1, 1), ("c", 2, 1, 2), ("c", 2, 2, 1), ("c", 2, 2, 2), ("r", 2),
-    ("c", 2, 0, 1), ("c", 2, 0, 2), ("c", 1, 1, 1), ("c", 1, 1, 2), ("c", 1, 2, 1), ("c", 1, 2, 2), ("r", 1),
-    ("c", 1, 0, 1), ("c", 1, 0, 2), ("n", 2), ("n", 1),
+    ("y", "kv", 0), ("f", 0, 0), ("y", "q", 0), ("y", "kv", 1), ("y", "q", 1), ("y", "kv", 2), ("y", "q", 2),
+    ("f", 0, 1), ("f", 0, 3), ("f", 0, 2), ("q", 0), ("f", 1, 0), ("f", 1, 1), ("f", 1, 3), ("f", 1, 2), ("q", 1),
+    ("rq", 1), ("text", 0), ("c", 0, 0, 0), ("c", 0, 1, 0), ("c", 0, 2, 0), ("fs", 0), ("f", 2, 0), ("f", 2, 1),
+    ("f", 2, 3), ("f", 2, 2), ("q", 2), ("c", 0, 1, 1), ("c", 0, 2, 1), ("c", 0, 1, 2), ("c", 0, 2, 2), ("r", 0),
+    ("c", 0, 0, 1), ("c", 0, 0, 2), ("text", 1), ("c", 1, 0, 0), ("c", 1, 1, 0), ("c", 1, 2, 0), ("c", 1, 1, 1),
+    ("c", 1, 2, 1), ("c", 1, 1, 2), ("c", 1, 2, 2), ("r", 1), ("ro", 1), ("n", 0), ("text", 2), ("c", 2, 0, 0),
+    ("c", 2, 1, 0), ("c", 2, 2, 0), ("c", 1, 0, 1), ("c", 1, 0, 2), ("c", 2, 1, 1), ("c", 2, 2, 1), ("c", 2, 1, 2),
+    ("c", 2, 2, 2), ("r", 2), ("c", 2, 0, 1), ("c", 2, 0, 2), ("n", 1), ("n", 2),
 )
 
 
 def kernel(
     grid_rows, nh, hd,
     qkv, text, mask, out,
-    q_s, kv_s, text_s, mask_s, bias_s, m_s, l_s, acc_s, osend_s, orecv_s, lsend_s, lrecv_s, ofin_s,
-    own_sem, kv_sem, q_sem, text_sem, a2a_send,
-    kv_send, kv_recv, q_send, q_recv, mk_send, mk_recv, o_send, o_recv, ls_send, ls_recv, out_send, out_sem,
+    q_s, kv_s, text_s, mask_s, mask_t, bias_s, m_s, l_s, acc_s, osend_s, orecv_s, lsend_s, lrecv_s, ofin_s, relay_q, relay_o,
+    kv_sem, q_sem, text_sem, a2a_send,
+    kv_send, kv_recv, q_send, q_recv, mk_send, mk_recv, o_send, o_recv, ls_send, ls_recv, out_send, out_sem, relay_sem,
 ):
     s, my = lax.axis_index("seq"), lax.axis_index("head")
-    row, col = s // GW, s % GW
     rows = qkv.shape[1]
     total = rows * nh
     tile = total // 2
     quarters = nh // CORES
     part = rows * CORES
     core, hi = my % CORES, my // CORES
+    half = grid_rows * GW // 2
+    lo, rest_s = s // half, s % half
+    c = core * half + rest_s
+    group = hi * 2 + lo
+    row, col = c // GW, c % GW
+    home = core == lo
+
+    def holder(column):
+        return (lo * half + column % half, hi * CORES + column // half)
+
     has = [[None, row > 0, row < grid_rows - 1], [None, col > 0, col < GW - 1]]
-    dev = [[None, (s - GW, my), (s + GW, my)], [None, (s - 1, my), (s + 1, my)]]
+    dev = [[None, holder(c - GW), holder(c + GW)], [None, holder(c - 1), holder(c + 1)]]
+    on_edge = [None, col == EDGE + 1, col == EDGE]
+
+    def relays(i):
+        return [(ROUTES[i][0], EDGE + 1, 1, EDGE), (ROUTES[i][1], EDGE, 2, EDGE + 1)] if i in ROUTES else []
+
     kv_axis = [MODES[i] for i in range(hd)]
     q_axis = [1 - MODES[i] for i in range(hd)]
-    mate = hi * CORES + 1 - core
-    far = [(r, ((hi + r) % quarters) * CORES + (core + o) % CORES) for r in range(1, quarters) for o in range(CORES)]
-    peers = [(0, mate)] + sorted(far, key=lambda p: 2 * p[0] == quarters)
+    steps = [0] + sorted(range(1, quarters), key=lambda t: 2 * t == quarters)
+    goes = []
+    for t in steps:
+        to = lax.rem(hi + quarters - t, quarters)
+        for l in (lo, 1 - lo):
+            goes.append((t, (l * half + rest_s, to * CORES + lo), to * 2 + l, t == 0 and l is lo))
+    owners = [(core * half + rest_s, j) for j in range(nh)]
     my_rows = pl.ds(pl.multiple_of(my * rows, rows), rows)
 
     def lanes(h, i, n=1):
@@ -67,15 +86,22 @@
     def wait(ref, sem):
         pltpu.make_async_copy(ref, ref, sem).wait()
 
-    pltpu.make_async_copy(qkv.at[pl.ds(1, 2), :, lanes(my, 0, hd)], kv_s.at[0, :, my_rows, :], own_sem).start()
-    for i in range(hd):
-        pltpu.make_async_copy(qkv.at[0, :, lanes(my, i)], q_s.at[0, my_rows, at(i)], q_sem.at[i]).start()
-    pltpu.make_async_copy(text, text_s, text_sem).start()
+    mate = (s, hi * CORES + 1 - core)
+    across = ((1 - lo) * half + rest_s, my)
 
     barrier = pltpu.get_barrier_semaphore()
-    count = len(peers)
-    for _, p in peers:
-        pl.semaphore_signal(barrier, inc=1, device_id=(s, p), device_id_type=MESH)
+    count = len(goes) + quarters - home.astype(jnp.int32)
+    for _, to, _, maybe in goes:
+        if maybe:
+            @pl.when(jnp.logical_not(home))
+            def _():
+                pl.semaphore_signal(barrier, inc=1, device_id=to, device_id_type=MESH)
+        else:
+            pl.semaphore_signal(barrier, inc=1, device_id=to, device_id_type=MESH)
+    for t in range(quarters):
+        pl.semaphore_signal(
+            barrier, inc=1, device_id=(core * half + rest_s, t * CORES + 1 - lo), device_id_type=MESH
+        )
     for a in (0, 1):
         for k in (1, 2):
             count = count + has[a][k].astype(jnp.int32)
@@ -83,29 +109,70 @@
             @pl.when(has[a][k])
             def _():
                 pl.semaphore_signal(barrier, inc=1, device_id=dev[a][k], device_id_type=MESH)
+
+    for i in ROUTES:
+        for at_col, to_col, slot, from_col in relays(i):
+            count = count + (col == from_col).astype(jnp.int32) + (col == at_col).astype(jnp.int32)
+
+            @pl.when(col == at_col)
+            def _():
+                pl.semaphore_signal(barrier, inc=1, device_id=holder(c - at_col + from_col), device_id_type=MESH)
+
+            @pl.when(col == to_col)
+            def _():
+                pl.semaphore_signal(barrier, inc=1, device_id=holder(c - to_col + at_col), device_id_type=MESH)
+
+    @pl.when(home)
+    def _():
+        pltpu.make_async_copy(text, text_s, text_sem).start()
+
+    mask_s[0] = jnp.zeros_like(mask_s[0])
+
+    @pl.when(home)
+    def _():
+        mask_s[0, 0:2, 0:27] = mask[...]
 
     m_s[...] = jnp.full_like(m_s, NEG)
     l_s[...] = jnp.zeros_like(l_s)
     acc_s[...] = jnp.zeros_like(acc_s)
     pl.semaphore_wait(barrier, count)
 
-    remote(qkv.at[pl.ds(1, 2), :, lanes(mate, 0, hd)], kv_s.at[0, :, my_rows, :], a2a_send.at[2, 0], own_sem, (s, mate))
+    @pl.when(home)
+    def _():
+        mask_t[0] = mask_s[0]
+        remote(mask_t.at[0], mask_t.at[1], mk_send.at[2, 0], mk_recv.at[2, 0], across)
+        remote(text, text_s, mk_send.at[2, 1], text_sem, mate)
 
     def send(kind, i):
-        for r, p in peers:
+        for t, to, g, maybe in goes:
             if kind == 0:
-                remote(qkv.at[0, :, lanes(p, i)], q_s.at[0, my_rows, at(i)], a2a_send.at[0, i], q_sem.at[i], (s, p))
-            elif r > 0:
-                remote(
-                    qkv.at[pl.ds(1, 2), :, lanes(p, i)], kv_s.at[0, :, my_rows, at(i)],
-                    a2a_send.at[1, i], kv_sem.at[i, quarters - r], (s, p),
-                )
+                src, dst = qkv.at[0, :, lanes(g, i)], q_s.at[0, my_rows, at(i)]
+                ssem, rsem = a2a_send.at[0, i], q_sem.at[i]
+            else:
+                src, dst = qkv.at[pl.ds(1, 2), :, lanes(g, i)], kv_s.at[0, :, my_rows, at(i)]
+                ssem, rsem = a2a_send.at[1, i], kv_sem.at[i, t]
+            if maybe:
+                @pl.when(home)
+                def _():
+                    pltpu.make_async_copy(src, dst, rsem).start()
+
+                @pl.when(jnp.logical_not(home))
+                def _():
+                    remote(src, dst, ssem, rsem, to)
+            else:
+                remote(src, dst, ssem, rsem, to)
 
     def sent(kind, i):
-        if kind == 0:
-            wait(q_s.at[0, pl.ds(0, total - rows), at(i)], a2a_send.at[0, i])
-        else:
-            wait(kv_s.at[0, :, pl.ds(0, total - part), at(i)], a2a_send.at[1, i])
+        sem = a2a_send.at[kind, i]
+        block_of = (lambda n: q_s.at[0, pl.ds(0, n), at(i)]) if kind == 0 else (lambda n: kv_s.at[0, :, pl.ds(0, n), at(i)])
+
+        @pl.when(home)
+        def _():
+            wait(block_of(total - rows), sem)
+
+        @pl.when(jnp.logical_not(home))
+        def _():
+            wait(block_of(total), sem)
 
     def make_bias(mode, qs):
         which = 0 if qs == 0 else 1 + 2 * (1 - mode) + qs - 1
@@ -123,8 +190,7 @@
     def forward_kv(i, back):
         g = (hi + back) % quarters
         where = pl.ds(pl.multiple_of(g * part, part), part)
-        if back > 0:
-            wait(kv_s.at[0, :, where, at(i)], kv_sem.at[i, back])
+        wait(kv_s.at[0, :, where, at(i)], kv_sem.at[i, back])
         a = kv_axis[i]
         for k in (1, 2):
             @pl.when(has[a][k])
@@ -144,9 +210,36 @@
         wait(q_s.at[0, :, at(i)], q_sem.at[i])
         a = q_axis[i]
         for k in (1, 2):
-            @pl.when(has[a][k])
-            def _():
-                remote(q_s.at[0, :, at(i)], q_s.at[3 - k, :, at(i)], q_send.at[i, k - 1], q_recv.at[i, 2 - k], dev[a][k])
+            src, ssem = q_s.at[0, :, at(i)], q_send.at[i, k - 1]
+
+            @pl.when(jnp.logical_and(has[a][k], jnp.logical_not(on_edge[k])) if i in ROUTES else has[a][k])
+            def _():
+                remote(src, q_s.at[3 - k, :, at(i)], ssem, q_recv.at[i, 2 - k], dev[a][k])
+
+        for at_col, to_col, slot, from_col in relays(i):
+            @pl.when(col == from_col)
+            def _():
+                remote(
+                    q_s.at[0, :, at(i)], relay_q, q_send.at[i, 2 - slot], relay_sem.at[0], holder(c - from_col + at_col)
+                )
+
+    def pass_q(i):
+        for at_col, to_col, slot, from_col in relays(i):
+            @pl.when(col == at_col)
+            def _():
+                wait(relay_q, relay_sem.at[0])
+                remote(
+                    relay_q, q_s.at[slot, :, at(i)], relay_sem.at[1], q_recv.at[i, slot - 1], holder(c - at_col + to_col)
+                )
+
+    def pass_o(i):
+        for at_col, to_col, slot, from_col in relays(i):
+            @pl.when(col == at_col)
+            def _():
+                wait(relay_o, relay_sem.at[2])
+                remote(
+                    relay_o, orecv_s.at[slot - 1, i], relay_sem.at[3], o_recv.at[i, slot - 1], holder(c - at_col + to_col)
+                )
 
     def forwarded_q(i):
         for k in (1, 2):
@@ -214,6 +307,13 @@
     def text_block(i):
         update(i, 0, text_s[0, :, at(i)], text_s[1, :, at(i)], [None] * (text_s.shape[1] // tile))
 
+    def remote_o(i, k):
+        @pl.when(jnp.logical_not(on_edge[k]) if i in ROUTES else has[1][k])
+        def _():
+            remote(
+                osend_s.at[k - 1, i], orecv_s.at[2 - k, i], o_send.at[i, k - 1], o_recv.at[i, 2 - k], dev[1][k]
+            )
+
     def give_back(i):
         a = q_axis[i]
         for k in (1, 2):
@@ -225,8 +325,16 @@
                 lsend_s[k - 1, i] = jnp.broadcast_to(
                     jnp.where(some, m_s[k, i] * C2 + jnp.log2(l), NEG), lsend_s.shape[2:]
                 )
-                remote(osend_s.at[k - 1, i], orecv_s.at[2 - k, i], o_send.at[i, k - 1], o_recv.at[i, 2 - k], dev[a][k])
+                remote_o(i, k)
                 remote(lsend_s.at[k - 1, i], lrecv_s.at[2 - k, i], ls_send.at[i, k - 1], ls_recv.at[i, 2 - k], dev[a][k])
+
+        for at_col, to_col, slot, from_col in relays(i):
+            @pl.when(col == from_col)
+            def _():
+                remote(
+                    osend_s.at[2 - slot, i], relay_o, o_send.at[i, 2 - slot], relay_sem.at[2],
+                    holder(c - from_col + at_col),
+                )
 
     def finish(i):
         a = q_axis[i]
@@ -251,16 +359,24 @@
         scale = 1.0 / (w + w1 + w2)
         o = acc_s[0, i] * (w * scale / l) + parts[0][1] * (w1 * scale) + parts[1][1] * (w2 * scale)
         ofin_s[:, at(i)] = o.T.astype(jnp.bfloat16)
-        for _, p in peers:
-            remote(
-                ofin_s.at[pl.ds(pl.multiple_of(p * rows, rows), rows), at(i)], out.at[:, lanes(my, i)],
-                out_send, out_sem, (s, p),
-            )
-        pltpu.make_async_copy(ofin_s.at[my_rows, at(i)], out.at[:, lanes(my, i)], out_sem).start()
+        for j, to in enumerate(owners):
+            src, dst = ofin_s.at[pl.ds(j * rows, rows), at(i)], out.at[:, lanes(group, i)]
+            mine = jnp.logical_and(home, my == j)
+
+            @pl.when(mine)
+            def _():
+                pltpu.make_async_copy(src, dst, out_sem).start()
+
+            @pl.when(jnp.logical_not(mine))
+            def _():
+                remote(src, dst, out_send, out_sem, to)
 
     def masks():
-        mask_s[0] = jnp.zeros_like(mask_s[0])
-        mask_s[0, 0:2, 0:27] = mask[...]
+        @pl.when(jnp.logical_not(home))
+        def _():
+            wait(mask_t.at[1], mk_recv.at[2, 0])
+            mask_s[0] = mask_t[1]
+
         for a in (0, 1):
             for k in (1, 2):
                 @pl.when(has[a][k])
@@ -288,8 +404,6 @@
         elif op == "f":
             if first:
                 first = False
-                own_part = pl.ds(pl.multiple_of(hi * part, part), part)
-                wait(kv_s.at[0, :, own_part, :], own_sem)
                 forward_kv(*rest)
                 masks()
                 biases()
@@ -308,10 +422,30 @@
             block(*rest)
         elif op == "r":
             give_back(rest[0])
+        elif op == "rq":
+            pass_q(rest[0])
+        elif op == "ro":
+            pass_o(rest[0])
         elif op == "n":
             finish(rest[0])
 
-    wait(kv_s.at[0, :, pl.ds(0, rows), :], a2a_send.at[2, 0])
+    @pl.when(home)
+    def _():
+        wait(mask_t.at[0], mk_send.at[2, 0])
+        wait(text_s, mk_send.at[2, 1])
+        wait(ofin_s.at[pl.ds(0, total - rows), :], out_send)
+
+    @pl.when(jnp.logical_not(home))
+    def _():
+        wait(ofin_s, out_send)
+
+    for i in ROUTES:
+        for at_col, to_col, slot, from_col in relays(i):
+            @pl.when(col == at_col)
+            def _():
+                wait(relay_q, relay_sem.at[1])
+                wait(relay_o, relay_sem.at[3])
+
     for i in range(hd):
         for kind, name in ((0, "q"), (1, "kv")):
             if ("ys", name, i) not in PLAN:
@@ -332,7 +466,6 @@
                 wait(mask_s.at[0], mk_send.at[a, k - 1])
                 if 1 - a not in MODES:
                     wait(mask_s.at[1 + 2 * a + k - 1], mk_recv.at[a, k - 1])
-    wait(ofin_s.at[pl.ds(0, total - rows), :], out_send)
     wait(out, out_sem)
 
 
@@ -362,6 +495,7 @@
                 pltpu.VMEM((3, 2, total, width), bf),
                 pltpu.VMEM((2, txt, width), bf),
                 pltpu.VMEM((5, 8, 128), jnp.int32),
+                pltpu.VMEM((2, 8, 128), jnp.int32),
                 pltpu.VMEM((2, 3, 3, 2, 1, total), F32),
                 pltpu.VMEM((3, hd, 1, total), F32),
                 pltpu.VMEM((3, hd, 1, total), F32),
@@ -371,9 +505,11 @@
                 pltpu.VMEM((2, hd, 8, total), F32),
                 pltpu.VMEM((2, hd, 8, total), F32),
                 pltpu.VMEM((total, width), bf),
-                dma, dma((hd, quarters)), dma((hd,)), dma, dma((3, hd)),
-                dma((hd, 2)), dma((hd, 2)), dma((hd, 2)), dma((hd, 2)), dma((2, 2)), dma((2, 2)),
-                dma((hd, 2)), dma((hd, 2)), dma((hd, 2)), dma((hd, 2)), dma, dma,
+                pltpu.VMEM((total, HEAD_DIM), bf),
+                pltpu.VMEM((HEAD_DIM, total), bf),
+                dma((hd, quarters)), dma((hd,)), dma, dma((2, hd)),
+                dma((hd, 2)), dma((hd, 2)), dma((hd, 2)), dma((hd, 2)), dma((3, 2)), dma((3, 2)),
+                dma((hd, 2)), dma((hd, 2)), dma((hd, 2)), dma((hd, 2)), dma, dma, dma((4,)),
             ],
             compiler_params=pltpu.CompilerParams(
                 collective_id=0, has_side_effects=True, vmem_limit_bytes=60 << 20

time: 101 us -> 81.9 us (0.81)
  the two profiles are of different devices: /device:TPU:15 before, /device:TPU:193 now
where the time goes in v3:
time: 81.9 us; the launch traced here: 81.6 us
  Pallas kernels  79.9 us (98%)
  local copies, waits for them, and re-layouts  1.77 us (2%)
    pallas_call x1, Pallas kernels, on_device(): pl.pallas_call(functools.partial(kernel, grid_rows, nh, hd), out_shape=ja...  79.9 us
    unnamed x1, local copies, waits for them, and re-layouts  1.77 us

profile of v3, /device:TPU:193, one launch (start us, length us, event | category | flops | bytes accessed | tf_op | source)
XLA Modules:
  0.0 81.6 jit_solution(10836641076027067481)
XLA Ops:
  0.0 79.9 %shard_map.37 = bf16[64,3072]{1,0:T(8,128)(2,1)} custom-call(bf16[3,64,3072]{2,1,0:T(8,128)(2,1)} %qkv.1, bf16[2,256,384]{2,1,0:T(8,128)(2,1)} %text.1, s32[2,27]{1,0:T(2,128)} %mask.1), custom_call_target="tpu_custom_call" | custom-call | flops 3825205248 | bytes 1572864 | tf_op jit(solution)/shard_map/pallas_call | solution.py:484
  79.9 1.8 %copy.5 = bf16[64,3072]{1,0:T(8,128)(2,1)} copy(bf16[64,3072]{1,0:T(8,128)(2,1)} %shard_map.37) | data formatting | bytes 786432

commit v4 on v3

--- a/solution.py
+++ b/solution.py
@@ -17,16 +17,15 @@
 F32 = jnp.float32
 MODES = (0, 0, 0)
 EDGE = GW // 2 - 1
-ROUTES = {1: (0, 7)}
+RELAYS = (0, 7)
+RELAY_Q = (0, 1)
+RELAY_O = (0,)
 PLAN = (
     ("y", "kv", 0), ("f", 0, 0), ("y", "q", 0), ("y", "kv", 1), ("y", "q", 1), ("y", "kv", 2), ("y", "q", 2),
-    ("f", 0, 1), ("f", 0, 3), ("f", 0, 2), ("q", 0), ("f", 1, 0), ("f", 1, 1), ("f", 1, 3), ("f", 1, 2), ("q", 1),
-    ("rq", 1), ("text", 0), ("c", 0, 0, 0), ("c", 0, 1, 0), ("c", 0, 2, 0), ("fs", 0), ("f", 2, 0), ("f", 2, 1),
-    ("f", 2, 3), ("f", 2, 2), ("q", 2), ("c", 0, 1, 1), ("c", 0, 2, 1), ("c", 0, 1, 2), ("c", 0, 2, 2), ("r", 0),
-    ("c", 0, 0, 1), ("c", 0, 0, 2), ("text", 1), ("c", 1, 0, 0), ("c", 1, 1, 0), ("c", 1, 2, 0), ("c", 1, 1, 1),
-    ("c", 1, 2, 1), ("c", 1, 1, 2), ("c", 1, 2, 2), ("r", 1), ("ro", 1), ("n", 0), ("text", 2), ("c", 2, 0, 0),
-    ("c", 2, 1, 0), ("c", 2, 2, 0), ("c", 1, 0, 1), ("c", 1, 0, 2), ("c", 2, 1, 1), ("c", 2, 2, 1), ("c", 2, 1, 2),
-    ("c", 2, 2, 2), ("r", 2), ("c", 2, 0, 1), ("c", 2, 0, 2), ("n", 1), ("n", 2),
+    ("f", 0, 1), ("f", 0, 3), ("f", 0, 2), ("q", 0), ("f", 1, 0), ("f", 1, 1), ("f", 1, 3), ("f", 1, 2), ("rq", 0),
+    ("q", 1), ("f", 2, 0), ("own", 0), ("f", 2, 1), ("f", 2, 3), ("f", 2, 2), ("q", 2), ("rq", 1), ("side", 0),
+    ("back", 0), ("r", 0), ("last", 0), ("own", 1), ("ro", 0), ("side", 1), ("back", 1), ("r", 1), ("n", 0),
+    ("own", 2), ("side", 2), ("back", 2), ("r", 2), ("last", 1), ("n", 1), ("last", 2), ("n", 2),
 )
 
 
@@ -58,8 +57,8 @@
     dev = [[None, holder(c - GW), holder(c + GW)], [None, holder(c - 1), holder(c + 1)]]
     on_edge = [None, col == EDGE + 1, col == EDGE]
 
-    def relays(i):
-        return [(ROUTES[i][0], EDGE + 1, 1, EDGE), (ROUTES[i][1], EDGE, 2, EDGE + 1)] if i in ROUTES else []
+    def relays(i, heads):
+        return [(RELAYS[0], EDGE + 1, 1, EDGE), (RELAYS[1], EDGE, 2, EDGE + 1)] if i in heads else []
 
     kv_axis = [MODES[i] for i in range(hd)]
     q_axis = [1 - MODES[i] for i in range(hd)]
@@ -110,17 +109,16 @@
             def _():
                 pl.semaphore_signal(barrier, inc=1, device_id=dev[a][k], device_id_type=MESH)
 
-    for i in ROUTES:
-        for at_col, to_col, slot, from_col in relays(i):
-            count = count + (col == from_col).astype(jnp.int32) + (col == at_col).astype(jnp.int32)
-
-            @pl.when(col == at_col)
-            def _():
-                pl.semaphore_signal(barrier, inc=1, device_id=holder(c - at_col + from_col), device_id_type=MESH)
-
-            @pl.when(col == to_col)
-            def _():
-                pl.semaphore_signal(barrier, inc=1, device_id=holder(c - to_col + at_col), device_id_type=MESH)
+    for at_col, to_col, slot, from_col in relays(0, (0,)):
+        count = count + (col == from_col).astype(jnp.int32) + (col == at_col).astype(jnp.int32)
+
+        @pl.when(col == at_col)
+        def _():
+            pl.semaphore_signal(barrier, inc=1, device_id=holder(c - at_col + from_col), device_id_type=MESH)
+
+        @pl.when(col == to_col)
+        def _():
+            pl.semaphore_signal(barrier, inc=1, device_id=holder(c - to_col + at_col), device_id_type=MESH)
 
     @pl.when(home)
     def _():
@@ -135,6 +133,16 @@
     m_s[...] = jnp.full_like(m_s, NEG)
     l_s[...] = jnp.zeros_like(l_s)
     acc_s[...] = jnp.zeros_like(acc_s)
+    for k in (1, 2):
+        @pl.when(jnp.logical_not(has[1][k]))
+        def _():
+            q_s[k] = jnp.zeros_like(q_s[k])
+            mask_s[2 + k] = jnp.zeros_like(mask_s[2 + k])
+
+        @pl.when(jnp.logical_not(has[0][k]))
+        def _():
+            kv_s[k] = jnp.zeros_like(kv_s[k])
+
     pl.semaphore_wait(barrier, count)
 
     @pl.when(home)
@@ -212,33 +220,35 @@
         for k in (1, 2):
             src, ssem = q_s.at[0, :, at(i)], q_send.at[i, k - 1]
 
-            @pl.when(jnp.logical_and(has[a][k], jnp.logical_not(on_edge[k])) if i in ROUTES else has[a][k])
+            @pl.when(jnp.logical_and(has[a][k], jnp.logical_not(on_edge[k])) if i in RELAY_Q else has[a][k])
             def _():
                 remote(src, q_s.at[3 - k, :, at(i)], ssem, q_recv.at[i, 2 - k], dev[a][k])
 
-        for at_col, to_col, slot, from_col in relays(i):
+        for at_col, to_col, slot, from_col in relays(i, RELAY_Q):
             @pl.when(col == from_col)
             def _():
                 remote(
-                    q_s.at[0, :, at(i)], relay_q, q_send.at[i, 2 - slot], relay_sem.at[0], holder(c - from_col + at_col)
+                    q_s.at[0, :, at(i)], relay_q.at[i], q_send.at[i, 2 - slot], relay_sem.at[0, i], holder(c - from_col + at_col)
                 )
 
     def pass_q(i):
-        for at_col, to_col, slot, from_col in relays(i):
+        for at_col, to_col, slot, from_col in relays(i, RELAY_Q):
             @pl.when(col == at_col)
             def _():
-                wait(relay_q, relay_sem.at[0])
+                wait(relay_q.at[i], relay_sem.at[0, i])
                 remote(
-                    relay_q, q_s.at[slot, :, at(i)], relay_sem.at[1], q_recv.at[i, slot - 1], holder(c - at_col + to_col)
+                    relay_q.at[i], q_s.at[slot, :, at(i)], relay_sem.at[1, i], q_recv.at[i, slot - 1],
+                    holder(c - at_col + to_col),
                 )
 
     def pass_o(i):
-        for at_col, to_col, slot, from_col in relays(i):
+        for at_col, to_col, slot, from_col in relays(i, RELAY_O):
             @pl.when(col == at_col)
             def _():
-                wait(relay_o, relay_sem.at[2])
+                wait(relay_o.at[i], relay_sem.at[2, i])
                 remote(
-                    relay_o, orecv_s.at[slot - 1, i], relay_sem.at[3], o_recv.at[i, slot - 1], holder(c - at_col + to_col)
+                    relay_o.at[i], orecv_s.at[slot - 1, i], relay_sem.at[3, i], o_recv.at[i, slot - 1],
+                    holder(c - at_col + to_col),
                 )
 
     def forwarded_q(i):
@@ -247,68 +257,75 @@
             def _():
                 wait(q_s.at[0, :, at(i)], q_send.at[i, k - 1])
 
-    def update(i, qs, k, v, biases):
-        q = q_s[qs, :, at(i)]
-        m_old = m_s[qs, i]
-        scores = []
-        m_new = m_old
-        for f, b in enumerate(biases):
-            sc = lax.dot_general(
-                k[f * tile:(f + 1) * tile], q, (((1,), (1,)), ((), ())), preferred_element_type=F32
-            )
-            top = jnp.max(sc, axis=0, keepdims=True)
-            m_new = jnp.maximum(m_new, top if b is None else top + b)
-            scores.append(sc)
-        alpha = jnp.exp2((m_old - m_new) * C2)
-        big = m_new * C2
-        l_new = l_s[qs, i] * alpha
-        acc = acc_s[qs, i] * alpha
-        for f, b in enumerate(biases):
-            sub = big if b is None else jnp.where(b < 0, -NEG, big)
-            e = jnp.exp2(scores[f] * C2 - sub)
-            l_new = l_new + jnp.sum(e, axis=0, keepdims=True)
-            acc = acc + lax.dot_general(
-                v[f * tile:(f + 1) * tile], e.astype(jnp.bfloat16), (((0,), (0,)), ((), ())),
-                preferred_element_type=F32,
-            )
-        m_s[qs, i] = m_new
-        l_s[qs, i] = l_new
-        acc_s[qs, i] = acc
+    def update(i, jobs):
+        scores, tops = [], []
+        for qs, tiles in jobs:
+            q = q_s[qs, :, at(i)]
+            m_new = m_s[qs, i]
+            mine = []
+            for k, v, b in tiles:
+                sc = lax.dot_general(k, q, (((1,), (1,)), ((), ())), preferred_element_type=F32)
+                top = jnp.max(sc, axis=0, keepdims=True)
+                m_new = jnp.maximum(m_new, top if b is None else top + b)
+                mine.append(sc)
+            scores.append(mine)
+            tops.append(m_new)
+        for (qs, tiles), mine, m_new in zip(jobs, scores, tops):
+            alpha = jnp.exp2((m_s[qs, i] - m_new) * C2)
+            big = m_new * C2
+            l_new = l_s[qs, i] * alpha
+            acc = acc_s[qs, i] * alpha
+            for (k, v, b), sc in zip(tiles, mine):
+                sub = big if b is None else jnp.where(b < 0, -NEG, big)
+                e = jnp.exp2(sc * C2 - sub)
+                l_new = l_new + jnp.sum(e, axis=0, keepdims=True)
+                acc = acc + lax.dot_general(
+                    v, e.astype(jnp.bfloat16), (((0,), (0,)), ((), ())), preferred_element_type=F32
+                )
+            m_s[qs, i] = m_new
+            l_s[qs, i] = l_new
+            acc_s[qs, i] = acc
 
     landed = set()
 
-    def block(i, qs, ks):
-        need_q, need_kv = qs and ("q", i, qs) not in landed, ks and ("kv", i, ks) not in landed
-        if need_q:
-            landed.add(("q", i, qs))
-
-            @pl.when(has[q_axis[i]][qs])
-            def _():
-                wait(q_s.at[qs, :, at(i)], q_recv.at[i, qs - 1])
-        if need_kv:
-            landed.add(("kv", i, ks))
-
-            @pl.when(has[kv_axis[i]][ks])
-            def _():
-                wait(kv_s.at[ks, :, :, at(i)], kv_recv.at[i, ks - 1])
-
-        def go():
-            update(
-                i, qs, kv_s[ks, 0, :, at(i)], kv_s[ks, 1, :, at(i)],
-                [bias_s[MODES[i], qs, ks, 0], bias_s[MODES[i], qs, ks, 1]],
-            )
-
-        guards = ([has[q_axis[i]][qs]] if qs else []) + ([has[kv_axis[i]][ks]] if ks else [])
-        if guards:
-            pl.when(functools.reduce(jnp.logical_and, guards))(go)
-        else:
-            go()
-
-    def text_block(i):
-        update(i, 0, text_s[0, :, at(i)], text_s[1, :, at(i)], [None] * (text_s.shape[1] // tile))
+    def tiles_of(i, qs, ks):
+        return [
+            (kv_s[ks, 0, f * tile:(f + 1) * tile, at(i)], kv_s[ks, 1, f * tile:(f + 1) * tile, at(i)],
+             bias_s[MODES[i], qs, ks, f])
+            for f in range(2)
+        ]
+
+    def attend(i, slots, parts):
+        for qs in slots:
+            if qs and ("q", i, qs) not in landed:
+                landed.add(("q", i, qs))
+
+                @pl.when(has[q_axis[i]][qs])
+                def _():
+                    wait(q_s.at[qs, :, at(i)], q_recv.at[i, qs - 1])
+        for ks in parts:
+            if ks and ("kv", i, ks) not in landed:
+                landed.add(("kv", i, ks))
+
+                @pl.when(has[kv_axis[i]][ks])
+                def _():
+                    wait(kv_s.at[ks, :, :, at(i)], kv_recv.at[i, ks - 1])
+        jobs = []
+        for qs in slots:
+            tiles = []
+            for ks in parts:
+                if ks is None:
+                    tiles += [
+                        (text_s[0, f * tile:(f + 1) * tile, at(i)], text_s[1, f * tile:(f + 1) * tile, at(i)], None)
+                        for f in range(text_s.shape[1] // tile)
+                    ]
+                else:
+                    tiles += tiles_of(i, qs, ks)
+            jobs.append((qs, tiles))
+        update(i, jobs)
 
     def remote_o(i, k):
-        @pl.when(jnp.logical_not(on_edge[k]) if i in ROUTES else has[1][k])
+        @pl.when(jnp.logical_not(on_edge[k]) if i in RELAY_O else has[1][k])
         def _():
             remote(
                 osend_s.at[k - 1, i], orecv_s.at[2 - k, i], o_send.at[i, k - 1], o_recv.at[i, 2 - k], dev[1][k]
@@ -328,11 +345,11 @@
                 remote_o(i, k)
                 remote(lsend_s.at[k - 1, i], lrecv_s.at[2 - k, i], ls_send.at[i, k - 1], ls_recv.at[i, 2 - k], dev[a][k])
 
-        for at_col, to_col, slot, from_col in relays(i):
+        for at_col, to_col, slot, from_col in relays(i, RELAY_O):
             @pl.when(col == from_col)
             def _():
                 remote(
-                    osend_s.at[2 - slot, i], relay_o, o_send.at[i, 2 - slot], relay_sem.at[2],
+                    osend_s.at[2 - slot, i], relay_o.at[i], o_send.at[i, 2 - slot], relay_sem.at[2, i],
                     holder(c - from_col + at_col),
                 )
 
@@ -392,7 +409,8 @@
                 @pl.when(has[1 - mode][k])
                 def _():
                     wait(mask_s.at[1 + 2 * (1 - mode) + k - 1], mk_recv.at[1 - mode, k - 1])
-                    make_bias(mode, k)
+
+                make_bias(mode, k)
 
     first = True
     kinds = {"q": 0, "kv": 1}
@@ -416,10 +434,14 @@
             forward_q(rest[0])
         elif op == "qs":
             forwarded_q(rest[0])
-        elif op == "text":
-            text_block(rest[0])
-        elif op == "c":
-            block(*rest)
+        elif op == "own":
+            attend(rest[0], (0,), (None, 0))
+        elif op == "side":
+            attend(rest[0], (1, 2), (0,))
+        elif op == "back":
+            attend(rest[0], (1, 2), (1, 2))
+        elif op == "last":
+            attend(rest[0], (0,), (1, 2))
         elif op == "r":
             give_back(rest[0])
         elif op == "rq":
@@ -439,12 +461,17 @@
     def _():
         wait(ofin_s, out_send)
 
-    for i in ROUTES:
-        for at_col, to_col, slot, from_col in relays(i):
+    for i in RELAY_Q:
+        for at_col, to_col, slot, from_col in relays(i, RELAY_Q):
             @pl.when(col == at_col)
             def _():
-                wait(relay_q, relay_sem.at[1])
-                wait(relay_o, relay_sem.at[3])
+                wait(relay_q.at[i], relay_sem.at[1, i])
+
+    for i in RELAY_O:
+        for at_col, to_col, slot, from_col in relays(i, RELAY_O):
+            @pl.when(col == at_col)
+            def _():
+                wait(relay_o.at[i], relay_sem.at[3, i])
 
     for i in range(hd):
         for kind, name in ((0, "q"), (1, "kv")):
@@ -505,11 +532,11 @@
                 pltpu.VMEM((2, hd, 8, total), F32),
                 pltpu.VMEM((2, hd, 8, total), F32),
                 pltpu.VMEM((total, width), bf),
-                pltpu.VMEM((total, HEAD_DIM), bf),
-                pltpu.VMEM((HEAD_DIM, total), bf),
+                pltpu.VMEM((hd, total, HEAD_DIM), bf),
+                pltpu.VMEM((hd, HEAD_DIM, total), bf),
                 dma((hd, quarters)), dma((hd,)), dma, dma((2, hd)),
                 dma((hd, 2)), dma((hd, 2)), dma((hd, 2)), dma((hd, 2)), dma((3, 2)), dma((3, 2)),
-                dma((hd, 2)), dma((hd, 2)), dma((hd, 2)), dma((hd, 2)), dma, dma, dma((4,)),
+                dma((hd, 2)), dma((hd, 2)), dma((hd, 2)), dma((hd, 2)), dma, dma, dma((4, hd)),
             ],
             compiler_params=pltpu.CompilerParams(
                 collective_id=0, has_side_effects=True, vmem_limit_bytes=60 << 20

time: 81.9 us -> 78.1 us (0.954)
  the two profiles are of different devices: /device:TPU:193 before, /device:TPU:151 now
where the time goes in v4:
time: 78.1 us; the launch traced here: 77.9 us
  Pallas kernels  76.1 us (97%)
  local copies, waits for them, and re-layouts  1.77 us (2%)
    pallas_call x1, Pallas kernels, on_device(): pl.pallas_call(functools.partial(kernel, grid_rows, nh, hd), out_shape=ja...  76.1 us
    unnamed x1, local copies, waits for them, and re-layouts  1.77 us

profile of v4, /device:TPU:151, one launch (start us, length us, event | category | flops | bytes accessed | tf_op | source)
XLA Modules:
  0.0 77.9 jit_solution(7601165099807599771)
XLA Ops:
  0.0 76.1 %shard_map.37 = bf16[64,3072]{1,0:T(8,128)(2,1)} custom-call(bf16[3,64,3072]{2,1,0:T(8,128)(2,1)} %qkv.1, bf16[2,256,384]{2,1,0:T(8,128)(2,1)} %text.1, s32[2,27]{1,0:T(2,128)} %mask.1), custom_call_target="tpu_custom_call" | custom-call | flops 3825205248 | bytes 1572864 | tf_op jit(solution)/shard_map/pallas_call | solution.py:511
  76.1 1.8 %copy.5 = bf16[64,3072]{1,0:T(8,128)(2,1)} copy(bf16[64,3072]{1,0:T(8,128)(2,1)} %shard_map.37) | data formatting | bytes 786432

commit v5 on v4

--- a/solution.py
+++ b/solution.py
@@ -516,7 +516,7 @@
                 pl.BlockSpec(memory_space=pl.ANY),
                 pl.BlockSpec(memory_space=pltpu.VMEM),
             ],
-            out_specs=pl.BlockSpec(memory_space=pltpu.VMEM),
+            out_specs=pl.BlockSpec(memory_space=pl.ANY),
             scratch_shapes=[
                 pltpu.VMEM((3, total, width), bf),
                 pltpu.VMEM((3, 2, total, width), bf),

time: 78.1 us -> 77.5 us (level)
  no operation moved by 1% of the time
where the time goes in v5:
time: 77.5 us; the launch traced here: 77.3 us
  Pallas kernels  75.5 us (97%)
  local copies, waits for them, and re-layouts  1.77 us (2%)
    pallas_call x1, Pallas kernels, on_device(): pl.pallas_call(functools.partial(kernel, grid_rows, nh, hd), out_shape=ja...  75.5 us
    unnamed x1, local copies, waits for them, and re-layouts  1.77 us

profile of v5, /device:TPU:151, one launch (start us, length us, event | category | flops | bytes accessed | tf_op | source)
XLA Modules:
  0.0 77.3 jit_solution(3629887781399414109)
XLA Ops:
  0.0 75.5 %shard_map.37 = bf16[64,3072]{1,0:T(8,128)(2,1)} custom-call(bf16[3,64,3072]{2,1,0:T(8,128)(2,1)} %qkv.1, bf16[2,256,384]{2,1,0:T(8,128)(2,1)} %text.1, s32[2,27]{1,0:T(2,128)} %mask.1), custom_call_target="tpu_custom_call" | custom-call | flops 3825205248 | bytes 1572864 | tf_op jit(solution)/shard_map/pallas_call | solution.py:511
  75.5 1.8 %copy.5 = bf16[64,3072]{1,0:T(8,128)(2,1)} copy(bf16[64,3072]{1,0:T(8,128)(2,1)} %shard_map.37) | data formatting | bytes 786432
